TPU v7x, 32 devices: a whole 2x2x4 slice. The times are simulated.
32 devices in a mesh: row: 8 (over y, x, core), col: 4 (over z).
Axes of the slice: x: 2, y: 2, z: 4, core: 2. Of those that a mesh axis runs over, the one named last changes fastest.
Arguments:
- block_out: bfloat16 [384, 8192], P('row', 'col'), may hold values from -250 to 250
- stream_mid: bfloat16 [384, 8192], P('row', 'col'), may hold values from -250 to 250
- gate_pre: bfloat16 [384, 28672], P('row', 'col'), may hold values from -8 to 8
- up_pre: bfloat16 [384, 28672], P('row', 'col'), may hold values from -6 to 6
- final_gain: float32 [8192], P('col'), may hold values from 0.28 to 1.72
- mlp_gain: float32 [8192], P('col'), may hold values from 0.1 to 1.9
- value_weight: float32 [8192], P('col'), may hold values from -0.006629126 to 0.006629126
- returns: float32 [384], P('row'), may hold values from -6 to 6
- response_mask: int32 [384], P('row'), may hold values from 0 to 1, as said below
- w_gate: bfloat16 [8192, 28672], P('row', 'col'), may hold values from -0.0625 to 0.0625
- w_up: bfloat16 [8192, 28672], P('row', 'col'), may hold values from -0.0625 to 0.0625
- w_down: bfloat16 [28672, 8192], P('col', 'row'), may hold values from -0.03125 to 0.03125
Outputs:
- stream_mid_gradient: bfloat16 [384, 8192], P('row', 'col')
- d_w_down: float32 [28672, 8192], P('col', 'row')
Inputs may be any that keep to these rules, and one draw needn't show every extreme that they name: `response_mask`: the last token of the micro-batch is a response token.
All inputs are finite; a program needn't handle non-finite values.
Results may differ from a plain program's by a relative error of at most 0.0075.
Values may be sent and summed in bfloat16 or wider, within the bound.
No kernel may reach another device: no remote copies, remote signals or barrier semaphores. Data moves between devices by JAX's collectives and lax.ppermute only.
A program may use at most 128 MiB of HBM per device.

v0:
```python
import functools
import math

import jax
import jax.numpy as jnp
from jax import lax
from jax.experimental import pallas as pl
from jax.experimental.pallas import tpu as pltpu
from jax.sharding import PartitionSpec as P

epsilon = 1e-05
LANES = 128
MIB = 1024 * 1024
F32 = jnp.float32
BF16 = jnp.bfloat16


def bits_of(n):
    return [1 << i for i in range(n.bit_length() - 1)]


def block_of(extent, most):
    best = LANES
    for size in range(LANES, most + 1, LANES):
        if extent % size == 0:
            best = size
    return best


ordered = []


def call(kernel, grid, ins, outs, shapes, args, scratch=(), limit=32, cost=None, aliases={}, after=()):
    after = list(after) + ordered[-1:]
    known, extra = len(ins), len(after)

    def body(*refs):
        kernel(*refs[:known], *refs[known + extra :])

    result = pl.pallas_call(
        body,
        grid=grid,
        in_specs=list(ins) + [pl.BlockSpec(memory_space=pl.ANY)] * extra,
        out_specs=outs,
        out_shape=shapes,
        scratch_shapes=list(scratch),
        input_output_aliases=aliases,
        compiler_params=pltpu.CompilerParams(
            dimension_semantics=("arbitrary",) * len(grid), vmem_limit_bytes=limit * MIB
        ),
        cost_estimate=cost,
    )(*args, *after)
    ordered[:] = jax.tree.leaves(result)[-1:]
    return result


def cost(flops, moved, special=0):
    return pl.CostEstimate(flops=int(flops), bytes_accessed=int(moved), transcendentals=int(special))


def whole(shape):
    return pl.BlockSpec(shape, lambda i: (0,) * len(shape))


def column(values, position):
    return values[:, position : position + 1]


def place(columns, rows):
    lane = lax.broadcasted_iota(jnp.int32, (rows, LANES), 1)
    out = jnp.zeros((rows, LANES), F32)
    for position, values in enumerate(columns):
        out = jnp.where(lane == position, values, out)
    return out


def reverse_links(q, links):
    out = q & 1
    for i in range(links):
        out = out | (((q >> (1 + i)) & 1) << (links - i))
    return out


def other_core(j, links):
    return reverse_links(2 * j, links) | 1


def relative(place_ref, k, d):
    return lax.bitwise_xor(lax.bitwise_xor(lax.div(place_ref[0], k), place_ref[1]), d) * k


def label(place_ref, q, links):
    return jnp.where(lax.rem(place_ref[0], 2) == 1, reverse_links(q, links), q)


def slot(place_ref, k, links, d, s):
    own = lax.bitwise_xor(lax.rem(place_ref[0], k), s)
    return label(place_ref, relative(place_ref, k, d) + own, links)


def head_kernel(gain_ref, weight_ref, live_ref, head_ref, count_ref):
    head_ref[...] = gain_ref[...] * weight_ref[...]
    count = jnp.sum(live_ref[...].astype(F32), axis=1, keepdims=True)
    count_ref[...] = jnp.broadcast_to(count, count_ref.shape)


def turn(values):
    pad = jnp.zeros((LANES - values.shape[0], LANES), F32)
    return jnp.transpose(jnp.concatenate([values, pad], axis=0))


def gradient_rows(rows_of, token, head):
    root, dvalue, product = (column(token, i) for i in range(3))
    return (root * (head * dvalue - rows_of * root * product)).astype(BF16)


def out_kernel(tokens, k, links, place_ref, returns_ref, live_ref, count_ref, came_ref, *refs):
    columns = (len(refs) - 2) // (2 + k)
    pieces, heads, outs = refs[:columns], refs[columns : 2 * columns], refs[2 * columns : -2]
    token_ref, held_ref = refs[-2:]
    own, block = pieces[0].shape
    width, tile = block * columns, block // k
    squares = products = jnp.zeros((own, 1), F32)
    for piece, head in zip(pieces, heads):
        wide = piece[...].astype(F32)
        squares = squares + jnp.sum(wide * wide, axis=1, keepdims=True)
        products = products + jnp.sum(wide * head[...], axis=1, keepdims=True)
    pad = jnp.zeros((1, LANES - own), F32)
    rows = [returns_ref[...], live_ref[...].astype(F32)]
    rows = [jnp.concatenate([row, pad], axis=1) for row in rows] + [jnp.zeros((6, LANES), F32)]
    rows = turn(jnp.concatenate(rows, axis=0))[0:own]
    factor = (tokens * math.sqrt(width)) / (count_ref[0:1, 0:1] + came_ref[0:1, 0:1])
    root = lax.rsqrt(squares / width + epsilon)
    value = root * products
    dvalue = column(rows, 1) * (value - column(rows, 0)) * factor
    token = place([root, dvalue, dvalue * value / width], own)
    token_ref[...] = token
    for d in range(columns):
        for s in range(k):
            part = slice(s * tile, (s + 1) * tile)
            held_ref[slot(place_ref, k, links, d, s)] = gradient_rows(
                pieces[d][:, part].astype(F32), token, heads[d][:, part]
            )
    for q, out in enumerate(outs):
        out[...] = held_ref[q]


def arrange_kernel(k, links, place_ref, *refs):
    came, (keep_ref, send_ref, held_ref) = refs[:-3], refs[-3:]
    for q, ref in enumerate(came):
        held_ref[q] = ref[...]
    for d in range(len(came) // k):
        for s in range(k):
            (send_ref if d % 2 else keep_ref)[d // 2 * k + s] = held_ref[slot(place_ref, k, links, d, s)]


def partial_kernel(links, d_out_ref, w_ref, keep_ref, send_ref):
    count, own, tile = d_out_ref.shape
    result = lax.dot_general(
        d_out_ref[...].reshape(count * own, tile),
        w_ref[...],
        (((1,), (1,)), ((), ())),
        preferred_element_type=F32,
    ).astype(BF16)
    result = result.reshape(count, own, -1)
    for j in range(count // 2):
        keep_ref[j] = result[2 * j]
        send_ref[j] = result[other_core(j, links)]


def add_kernel(bit, keep_ref, came_ref, *outs):
    sent = kept = 0
    for q in range(keep_ref.shape[0]):
        total = (keep_ref[q].astype(F32) + came_ref[q].astype(F32)).astype(BF16)
        if len(outs) == 2 and q & bit:
            outs[1][sent] = total
            sent += 1
        else:
            outs[0][kept] = total
            kept += 1


def add(keep, came, bit, after=()):
    count, own, extent = keep.shape
    fb = block_of(extent, 2048 if count < 4 else 1024)
    block = pl.BlockSpec((count, own, fb), lambda i: (0, 0, i))
    parts = 2 if bit else 1
    out = pl.BlockSpec((count // parts, own, fb), lambda i: (0, 0, i))
    return call(
        functools.partial(add_kernel, bit),
        (extent // fb,),
        [block, block],
        [out] * parts,
        [jax.ShapeDtypeStruct((count // parts, own, extent), BF16)] * parts,
        [keep, came],
        cost=cost(count * own * extent, 6 * count * own * extent),
        after=after,
    )


def join_kernel(picks, *refs):
    for at, (i, j) in enumerate(picks):
        refs[-1][at] = refs[i][j]


def join(arrays, picks, after=()):
    own, extent = arrays[0].shape[1:]
    fb = block_of(extent, 1024)
    return call(
        functools.partial(join_kernel, picks),
        (extent // fb,),
        [pl.BlockSpec((array.shape[0], own, fb), lambda i: (0, 0, i)) for array in arrays],
        pl.BlockSpec((len(picks), own, fb), lambda i: (0, 0, i)),
        jax.ShapeDtypeStruct((len(picks), own, extent), BF16),
        arrays,
        cost=cost(0, 4 * len(picks) * own * extent),
        after=after,
    )


def every(*arrays):
    return [(i, j) for i, array in enumerate(arrays) for j in range(array.shape[0])]


def stack_kernel(count, *refs):
    for out in refs[count:]:
        for at in range(out.shape[0]):
            out[at] = refs[at][...]


def stack(arrays, own, counts, after=(), limit=32):
    extent = arrays[0].shape[1]
    fb = block_of(extent, 2048)
    return call(
        functools.partial(stack_kernel, len(arrays)),
        (extent // fb,),
        [pl.BlockSpec((own, fb), lambda i: (0, i))] * len(arrays),
        [pl.BlockSpec((count, own, fb), lambda i: (0, 0, i)) for count in counts],
        [jax.ShapeDtypeStruct((count, own, extent), BF16) for count in counts],
        arrays,
        cost=cost(0, 4 * len(arrays) * own * extent),
        after=after,
        limit=limit,
    )


def weight_kernel(links, picks, held, d_out_ref, *refs):
    out_ref, done_ref = refs[-2:]
    mine, other = refs[:held], refs[held : 2 * held]
    count, own, tile = d_out_ref.shape
    hidden = [None] * count
    for j in range(count // 2):
        for pair, position in ((mine, 2 * j), (other, other_core(j, links))):
            gate, up = (pair[i][at].astype(F32) for i, at in picks[j])
            hidden[position] = (gate * jax.nn.sigmoid(gate) * up).astype(BF16)
    out_ref[...] = lax.dot_general(
        jnp.concatenate(hidden, axis=0),
        d_out_ref[...].reshape(count * own, tile),
        (((0,), (0,)), ((), ())),
        preferred_element_type=F32,
    )
    done_ref[...] = jnp.zeros_like(done_ref)


def normed_kernel(links, picks, held, first, last, w_gate_ref, w_up_ref, *refs):
    total = refs[-1]
    outs = refs[2 * held + (2 if first else 3) : -1]
    mine, other = refs[:held], refs[held : 2 * held]
    mine_grad, other_grad = refs[2 * held : 2 * held + 2]
    before = None if first else refs[2 * held + 2]
    count, own = 2 * mine_grad.shape[0], mine_grad.shape[1]
    step = pl.program_id(0)

    d_gates, d_ups = [None] * count, [None] * count
    for j in range(count // 2):
        for pair, grad, position in (
            (mine, mine_grad, 2 * j),
            (other, other_grad, other_core(j, links)),
        ):
            gate, up = (pair[i][at].astype(F32) for i, at in picks[j])
            sig = jax.nn.sigmoid(gate)
            through = grad[j].astype(F32) * sig
            d_gates[position] = (through * up * (1.0 + gate * (1.0 - sig))).astype(BF16)
            d_ups[position] = (through * gate).astype(BF16)
    contracted = (((1,), (1,)), ((), ()))
    result = lax.dot_general(
        jnp.concatenate(d_gates, axis=0), w_gate_ref[...], contracted, preferred_element_type=F32
    ) + lax.dot_general(
        jnp.concatenate(d_ups, axis=0), w_up_ref[...], contracted, preferred_element_type=F32
    )

    @pl.when(step == 0)
    def _():
        total[...] = result if first else before[...] + result

    @pl.when(step > 0)
    def _():
        total[...] += result

    @pl.when(step == pl.num_programs(0) - 1)
    def _():
        if not last:
            outs[0][...] = total[...]
        else:
            for q, out in enumerate(outs):
                out[...] = total[q * own : (q + 1) * own, :].astype(BF16)


def product_kernel(mid_ref, gain_ref, back_ref, sums_ref):
    k, own, tile = back_ref.shape
    products = squares = jnp.zeros((own, 1), F32)
    for s in range(k):
        part = slice(s * tile, (s + 1) * tile)
        middle = mid_ref[:, part].astype(F32)
        products = products + jnp.sum(
            back_ref[s].astype(F32) * gain_ref[:, part] * middle, axis=1, keepdims=True
        )
        squares = squares + jnp.sum(middle * middle, axis=1, keepdims=True)
    sums_ref[...] = place([products, squares], own)


def pair_kernel(first_ref, second_ref, out_ref):
    out_ref[...] = first_ref[...] + second_ref[...]


def result_kernel(
    width, block_ref, mid_ref, head_ref, gain_ref, token_ref, sums_ref, came_ref, back_ref, out_ref
):
    k, own, tile = back_ref.shape
    sums = sums_ref[...] + came_ref[...]
    root = lax.rsqrt(column(sums, 1) / width + epsilon)
    product = column(sums, 0) * root / width
    for s in range(k):
        part = slice(s * tile, (s + 1) * tile)
        own_d_out = gradient_rows(block_ref[:, part].astype(F32), token_ref[...], head_ref[:, part])
        scaled = back_ref[s].astype(F32) * gain_ref[:, part]
        normalized = mid_ref[:, part].astype(F32) * root
        out_ref[:, part] = (own_d_out.astype(F32) + root * (scaled - normalized * product)).astype(BF16)


def local(
    block_out,
    stream_mid,
    gate_pre,
    up_pre,
    final_gain,
    mlp_gain,
    value_weight,
    returns,
    response_mask,
    w_gate,
    w_up,
    w_down,
):
    rows, cols = lax.axis_size("row"), lax.axis_size("col")
    k = rows // cols
    own, block = block_out.shape
    width = block * cols
    tile = width // rows
    units = gate_pre.shape[1]
    ordered.clear()
    where = jnp.stack([lax.axis_index("row"), lax.axis_index("col")]).astype(jnp.int32)
    smem = pl.BlockSpec(memory_space=pltpu.SMEM)
    final_gain, mlp_gain, value_weight = final_gain[None, :], mlp_gain[None, :], value_weight[None, :]

    link_bits = bits_of(rows)[1:]
    links = len(link_bits)

    def across(values, bit):
        return lax.ppermute(values, "row", [(r, r ^ bit) for r in range(rows)])

    def linked(values, i):
        pairs = [(r, r ^ link_bits[links - 1 - i if r % 2 else i]) for r in range(rows)]
        return lax.ppermute(values, "row", pairs)

    def along(values, bit):
        return lax.ppermute(values, "col", [(c, c ^ bit) for c in range(cols)])

    def exchanged(tiles):
        came = {0: tiles[0]}
        for q in range(1, rows):
            pairs = [(r, r ^ (reverse_links(q, links) if r % 2 else q)) for r in range(rows)]
            came[reverse_links(q, links) if q % 2 else q] = lax.ppermute(tiles[q], "row", pairs)
        return [came[q] for q in range(rows)]

    line = jax.ShapeDtypeStruct((8, LANES), F32)
    mask = response_mask[None, :]
    head, tally = call(
        head_kernel,
        (1,),
        [whole((1, block)), whole((1, block)), whole((1, own))],
        [whole((1, block)), whole((8, LANES))],
        [jax.ShapeDtypeStruct((1, block), F32), line],
        [final_gain, value_weight, mask],
        cost=cost(block, block * 12),
    )
    heads = [head] + [along(head, d) for d in range(1, cols)]
    pieces = [block_out] + [along(block_out, d) for d in range(1, cols)]
    for bit in link_bits:
        tally = call(
            pair_kernel,
            (1,),
            [whole((8, LANES))] * 2,
            whole((8, LANES)),
            line,
            [tally, across(tally, bit)],
            cost=cost(8 * LANES, 8 * LANES * 12),
        )

    paired, gate_own = stack([gate_pre, up_pre], own, [2, 1], after=heads[1:], limit=60)
    hop_a = linked(paired, 0)
    gate_b = linked(gate_own, 1)

    *tiles, token = call(
        functools.partial(out_kernel, own * rows, k, links),
        (1,),
        [smem, whole((1, own)), whole((1, own)), whole((8, LANES)), whole((8, LANES))]
        + [whole((own, block))] * cols
        + [whole((1, block))] * cols,
        [whole((own, tile))] * rows + [whole((own, LANES))],
        [jax.ShapeDtypeStruct((own, tile), BF16)] * rows + [jax.ShapeDtypeStruct((own, LANES), F32)],
        [where, returns[None, :], mask, tally, across(tally, 1), *pieces, *heads],
        scratch=[pltpu.VMEM((rows, own, tile), BF16)],
        cost=cost(own * width * 10, own * width * 4),
    )
    (d_out,) = stack(exchanged(tiles), own, [rows], after=[hop_a, gate_b])

    paired, hop_a, gate_b, up_late, d_out = lax.optimization_barrier(
        (paired, hop_a, gate_b, up_pre[None], d_out)
    )
    up_b = linked(up_late, 1)
    held = [paired, hop_a, gate_b, up_b, linked(hop_a, 1)]
    picks = [((0, 0), (0, 1)), ((1, 0), (1, 1)), ((2, 0), (3, 0)), ((4, 0), (4, 1))]
    for i in range(2, links):
        picks = picks + [tuple((at + len(held), j) for at, j in pair) for pair in picks]
        held = held + [linked(values, i) for values in held]
    others = [across(values, 1) for values in held]

    lines = units // (2 * LANES)
    sizes = [lines // 3, lines // 3]
    sizes = [size * 2 * LANES for size in sizes + [lines - sum(sizes)]]
    chunks = [(sum(sizes[:i]), size) for i, size in enumerate(sizes)]
    count = rows // 2

    def reduced(number):
        start, extent = chunks[number]
        fb = block_of(math.gcd(start, extent), 1024)
        keep, send = call(
            functools.partial(partial_kernel, links),
            (extent // fb,),
            [
                whole((rows, own, tile)),
                pl.BlockSpec((fb, tile), lambda i, f=start // fb: (f + i, 0)),
            ],
            [pl.BlockSpec((count, own, fb), lambda i: (0, 0, i))] * 2,
            [jax.ShapeDtypeStruct((count, own, extent), BF16)] * 2,
            [d_out, w_down],
            limit=47,
            cost=cost(2 * rows * own * tile * extent, 2 * extent * tile + 2 * rows * own * extent),
            after=waits.get((number, 0), ()),
        )
        received = across(send, 1)
        yield
        for i in range(links):
            keep, send = add(keep, received, 1, waits.get((number, 1 + i), ()))
            received = linked(send, i)
            yield
        (keep,) = add(keep, received, 0, waits.get((number, links + 1), ()))
        for i in range(links):
            came = linked(keep, i)
            yield
            keep = join([keep, came], every(keep, came), waits.get((number, links + 2 + i), ()))
        grads[number] = (keep, across(keep, 1))
        yield

    def normed(number, total):
        start, extent = chunks[number]
        first, last = number == 0, number == len(chunks) - 1
        fb = block_of(math.gcd(start, extent), 1024)
        weights = pl.BlockSpec((tile, fb), lambda i, f=start // fb: (0, f + i))
        ins = (
            [weights, weights]
            + [
                pl.BlockSpec((values.shape[0], own, fb), lambda i, f=start // fb: (0, 0, f + i))
                for values in held + others
            ]
            + [pl.BlockSpec((count, own, fb), lambda i: (0, 0, i))] * 2
        )
        args = [w_gate, w_up, *held, *others, *grads[number]]
        if not first:
            ins.append(whole((rows * own, tile)))
            args.append(total)
        shape, kind, parts = ((own, tile), BF16, rows) if last else ((rows * own, tile), F32, 1)
        result = call(
            functools.partial(normed_kernel, links, picks, len(held), first, last),
            (extent // fb,),
            ins,
            [whole(shape)] * parts,
            [jax.ShapeDtypeStruct(shape, kind)] * parts,
            args,
            scratch=[pltpu.VMEM((rows * own, tile), F32)],
            limit=36,
            cost=cost(
                4 * rows * own * tile * extent,
                4 * extent * tile + 6 * rows * own * extent,
                rows * own * extent,
            ),
        )
        return result if last else result[0]

    waits = {
        (1, 0): others[:3],
        (2, 0): held[3:5],
        (1, links): others[4:5],
        (0, links + 2): others[3:4],
    }
    grads, total = {}, None
    chains = [reduced(number) for number in range(len(chunks))]
    stages = 2 * links + 2
    for t in range(stages + len(chunks)):
        at = {number: t - number for number in range(len(chunks)) if 0 <= t - number <= stages}
        for number in sorted(at, key=lambda number: (at[number] == stages, -number)):
            if at[number] < stages:
                next(chains[number])
            else:
                total = normed(number, total)

    keep, send = call(
        functools.partial(arrange_kernel, k, links),
        (1,),
        [smem] + [whole((own, tile))] * rows,
        [whole((count, own, tile))] * 2,
        [jax.ShapeDtypeStruct((count, own, tile), BF16)] * 2,
        [where, *exchanged(total)],
        scratch=[pltpu.VMEM((rows, own, tile), BF16)],
        cost=cost(0, rows * own * tile * 4),
    )
    half = units // 2
    fb = block_of(half, 1024)
    blocks = half // fb
    d_w_down = None
    col_bits = bits_of(cols)
    for at, bit in enumerate(col_bits):
        received = along(send, bit)
        if at < 2:
            ins = [whole((rows, own, tile))] + [
                pl.BlockSpec((values.shape[0], own, fb), lambda i, at=at: (0, 0, at * blocks + i))
                for values in held + others
            ]
            args = [d_out, *held, *others]
            aliases = {}
            if at:
                ins.append(pl.BlockSpec(memory_space=pl.ANY))
                args.append(d_w_down)
                aliases = {len(args) - 1: 0}
            d_w_down, _ = call(
                functools.partial(weight_kernel, links, picks, len(held)),
                (blocks,),
                ins,
                [pl.BlockSpec((fb, tile), lambda i, at=at: (at * blocks + i, 0)), whole((8, LANES))],
                [jax.ShapeDtypeStruct((units, tile), F32), jax.ShapeDtypeStruct((8, LANES), F32)],
                args,
                cost=cost(
                    2 * rows * own * tile * half,
                    4 * half * tile + 4 * rows * own * half,
                    rows * own * half,
                ),
                aliases=aliases,
                limit=36,
            )
        if bit == col_bits[-1]:
            (total,) = add(keep, received, 0)
        else:
            keep, send = add(keep, received, k)

    row_spec, gain_spec = whole((own, block)), whole((1, block))
    sums_spec, back_spec = whole((own, LANES)), whole((k, own, tile))
    sums = call(
        product_kernel,
        (1,),
        [row_spec, gain_spec, back_spec],
        sums_spec,
        jax.ShapeDtypeStruct((own, LANES), F32),
        [stream_mid, mlp_gain, total],
        cost=cost(own * block * 5, own * block * 4),
    )
    for bit in col_bits[:-1]:
        sums = call(
            pair_kernel,
            (1,),
            [sums_spec] * 2,
            sums_spec,
            jax.ShapeDtypeStruct((own, LANES), F32),
            [sums, along(sums, bit)],
            cost=cost(own * LANES, own * LANES * 12),
        )
    gradient = call(
        functools.partial(result_kernel, width),
        (1,),
        [row_spec, row_spec, gain_spec, gain_spec] + [sums_spec] * 3 + [back_spec],
        row_spec,
        jax.ShapeDtypeStruct((own, block), BF16),
        [block_out, stream_mid, head, mlp_gain, token, sums, along(sums, col_bits[-1]), total],
        cost=cost(own * block * 14, own * block * 8),
    )
    return (gradient, d_w_down)


def solution(mesh):
    placed = (
        P("row", "col"),
        P("row", "col"),
        P("row", "col"),
        P("row", "col"),
        P("col"),
        P("col"),
        P("col"),
        P("row"),
        P("row"),
        P("row", "col"),
        P("row", "col"),
        P("col", "row"),
    )
    return jax.shard_map(
        local,
        mesh=mesh,
        in_specs=placed,
        out_specs=(P("row", "col"), P("col", "row")),
        check_vma=False,
    )
```

profile of v0, /device:TPU:4, one launch (start us, length us, event | category | flops | bytes accessed | tf_op | source)
XLA Modules:
  0.0 215.5 jit_solution(17815854286707832542)
XLA Ops:
  4.3 3.6 %collective-permute-start.8 = (f32[1,2048]{1,0:T(1,128)S(1)}, f32[1,2048]{1,0:T(1,128)S(1)}, u32[]{:S(2)}, u32[]{:S(2)}) collective-permute-start(f32[1,2048]{1,0:T(1,128)S(1)} %get-tuple-element.54.refs_9_.refs_2_), channel_id=1, source_target_pairs={{0,3},{1,2},{2,1},{3,0},{4,7},{5,6},{6,5},{7,4},{8,11},{9,10},{10,... | collective-permute-start | bytes 24584 | tf_op jit(solution)/shard_map/ppermute | solution.py:377
  14.1 3.7 %shard_map.134 = (bf16[2,48,7168]{2,1,0:T(8,128)(2,1)}, bf16[1,48,7168]{2,1,0:T(8,128)(2,1)}) custom-call(bf16[48,7168]{1,0:T(8,128)(2,1)} %refs_0_.6, bf16[48,7168]{1,0:T(8,128)(2,1)} %refs_1_.8, f32[1,2048]{1,0:T(1,128)} %copy-done.11, f32[1,2048]{1,0:T(1,128)} %copy-done.9, f32[1,2048]{1,0:T(1,128)} %copy-done.7, f32[8,128]{1,0:T(8,128)} %copy-done.4), custom_call_target="tpu_custom_call" | custom-call | bytes 2752512 | tf_op jit(solution)/shard_map/pallas_call | solution.py:40
  18.6 3.8 %collective-permute-start.5 = (bf16[48,2048]{1,0:T(8,128)(2,1)}, bf16[48,2048]{1,0:T(8,128)(2,1)S(1)}, u32[]{:S(2)}, u32[]{:S(2)}) collective-permute-start(bf16[48,2048]{1,0:T(8,128)(2,1)} %refs_0_.11), channel_id=1, source_target_pairs={{0,3},{1,2},{2,1},{3,0},{4,7},{5,6},{6,5},{7,4},{8,11},{9,10},{10,... | collective-permute-start | bytes 589832 | tf_op jit(solution)/shard_map/ppermute | solution.py:377
  23.1 5.5 %collective-permute-done.5.refs_8_ = bf16[48,2048]{1,0:T(8,128)(2,1)S(1)} collective-permute-done((bf16[48,2048]{1,0:T(8,128)(2,1)}, bf16[48,2048]{1,0:T(8,128)(2,1)S(1)}, u32[]{:S(2)}, u32[]{:S(2)}) %collective-permute-start.5) | collective-permute-done | bytes 196640 | tf_op jit(solution)/shard_map/ppermute | solution.py:377
  28.6 11.1 %collective-permute-done.4.refs_7_ = bf16[48,2048]{1,0:T(8,128)(2,1)S(1)} collective-permute-done((bf16[48,2048]{1,0:T(8,128)(2,1)}, bf16[48,2048]{1,0:T(8,128)(2,1)S(1)}, u32[]{:S(2)}, u32[]{:S(2)}) %collective-permute-start.4) | collective-permute-done | bytes 196640 | tf_op jit(solution)/shard_map/ppermute | solution.py:377
  55.4 4.7 %collective-permute-done.16.refs_6_ = bf16[48,1024]{1,0:T(8,128)(2,1)S(1)} collective-permute-done((bf16[48,1024]{1,0:T(8,128)(2,1)S(1)}, bf16[48,1024]{1,0:T(8,128)(2,1)S(1)}, u32[]{:S(2)}, u32[]{:S(2)}) %collective-permute-start.16) | collective-permute-done | bytes 98336 | tf_op jit(solution)/shard_map/ppermute | solution.py:383
  64.1 5.3 %shard_map.137 = (bf16[4,48,2304]{2,1,0:T(8,128)(2,1)S(1)}, bf16[4,48,2304]{2,1,0:T(8,128)(2,1)}) custom-call(bf16[8,48,1024]{2,1,0:T(8,128)(2,1)S(1)} %shard_map.136.refs_0_.refs_2_, bf16[7168,1024]{1,0:T(8,128)(2,1)} %refs_1_.11, bf16[8,48,1024]{2,1,0:T(8,128)(2,1)S(1)} %shard_map.136.refs_0_.refs_2_), custom_call_target="tpu_custom_call" | custom-call | flops 1811939328 | bytes 6488064 | tf_op jit(solution)/shard_map/pallas_call | solution.py:40
  70.6 5.3 %shard_map.138 = (bf16[4,48,2304]{2,1,0:T(8,128)(2,1)S(1)}, bf16[4,48,2304]{2,1,0:T(8,128)(2,1)}) custom-call(bf16[8,48,1024]{2,1,0:T(8,128)(2,1)S(1)} %shard_map.136.refs_0_.refs_2_, bf16[7168,1024]{1,0:T(8,128)(2,1)} %refs_1_.11, bf16[2,48,7168]{2,1,0:T(8,128)(2,1)S(1)} %collective-permute-done.20.refs_2_.refs_7_.refs_6_, ...), custom_call_target="tpu_custom_call" | custom-call | flops 1811939328 | bytes 6488064 | tf_op jit(solution)/shard_map/pallas_call | solution.py:40
  76.2 4.9 %collective-permute-done.19.refs_3_.refs_6_.refs_5_ = bf16[2,48,7168]{2,1,0:T(8,128)(2,1)S(1)} collective-permute-done((bf16[2,48,7168]{2,1,0:T(8,128)(2,1)S(1)}, bf16[2,48,7168]{2,1,0:T(8,128)(2,1)S(1)}, u32[]{:S(2)}, u32[]{:S(2)}) %collective-permute-start.19) | collective-permute-done | bytes 1376288 | tf_op jit(solution)/shard_map/ppermute | solution.py:374
  81.5 6.9 %collective-permute-done.18.refs_2_.refs_5_.refs_4_ = bf16[1,48,7168]{2,1,0:T(8,128)(2,1)S(1)} collective-permute-done((bf16[1,48,7168]{2,1,0:T(8,128)(2,1)S(1)}, bf16[1,48,7168]{2,1,0:T(8,128)(2,1)S(1)}, u32[]{:S(2)}, u32[]{:S(2)}) %collective-permute-start.18) | collective-permute-done | bytes 688160 | tf_op jit(solution)/shard_map/ppermute | solution.py:374
  88.4 5.6 %shard_map.140 = (bf16[4,48,2560]{2,1,0:T(8,128)(2,1)S(1)}, bf16[4,48,2560]{2,1,0:T(8,128)(2,1)S(1)}) custom-call(bf16[8,48,1024]{2,1,0:T(8,128)(2,1)S(1)} %shard_map.136.refs_0_.refs_2_, bf16[7168,1024]{1,0:T(8,128)(2,1)} %refs_1_.11, bf16[1,48,7168]{2,1,0:T(8,128)(2,1)S(1)} %collective-permute-done.18.refs_2_.refs_5_.refs_4_, ...), custom_call_target="tpu_custom_call" | custom-call | flops 2013265920 | bytes 7208960 | tf_op jit(solution)/shard_map/pallas_call | solution.py:40
  99.1 3.4 %collective-permute-done.27.refs_1_ = bf16[2,48,2304]{2,1,0:T(8,128)(2,1)S(1)} collective-permute-done((bf16[2,48,2304]{2,1,0:T(8,128)(2,1)S(1)}, bf16[2,48,2304]{2,1,0:T(8,128)(2,1)S(1)}, u32[]{:S(2)}, u32[]{:S(2)}) %collective-permute-start.27) | collective-permute-done | bytes 442400 | tf_op jit(solution)/shard_map/ppermute | solution.py:374
  108.6 4.8 %collective-permute-done.30.refs_1_ = bf16[1,48,2304]{2,1,0:T(8,128)(2,1)S(1)} collective-permute-done((bf16[1,48,2304]{2,1,0:T(8,128)(2,1)S(1)}, bf16[1,48,2304]{2,1,0:T(8,128)(2,1)S(1)}, u32[]{:S(2)}, u32[]{:S(2)}) %collective-permute-start.30) | collective-permute-done | bytes 221216 | tf_op jit(solution)/shard_map/ppermute | solution.py:374
  123.5 9.7 %collective-permute-done.32.refs_1_ = bf16[1,48,2560]{2,1,0:T(8,128)(2,1)S(1)} collective-permute-done((bf16[1,48,2560]{2,1,0:T(8,128)(2,1)S(1)}, bf16[1,48,2560]{2,1,0:T(8,128)(2,1)S(1)}, u32[]{:S(2)}, u32[]{:S(2)}) %collective-permute-start.32) | collective-permute-done | bytes 245792 | tf_op jit(solution)/shard_map/ppermute | solution.py:374
  136.5 7.3 %collective-permute-done.35.refs_1_ = bf16[1,48,2560]{2,1,0:T(8,128)(2,1)S(1)} collective-permute-done((bf16[1,48,2560]{2,1,0:T(8,128)(2,1)S(1)}, bf16[1,48,2560]{2,1,0:T(8,128)(2,1)S(1)}, u32[]{:S(2)}, u32[]{:S(2)}) %collective-permute-start.35) | collective-permute-done | bytes 245792 | tf_op jit(solution)/shard_map/ppermute | solution.py:374
  145.5 7.3 %shard_map.154.refs_2_.refs_14_ = f32[384,1024]{1,0:T(8,128)S(1)} custom-call(bf16[1024,7168]{1,0:T(8,128)(2,1)} %refs_0_.9, bf16[1024,7168]{1,0:T(8,128)(2,1)} %refs_1_.14, bf16[2,48,7168]{2,1,0:T(8,128)(2,1)S(1)} %copy-done, bf16[2,48,7168]{2,1,0:T(8,128)(2,1)S(1)} %collective-permute-done.9.refs_8_.refs_3_.refs_2_, ...), custom_call_target="tpu_custom_call" | custom-call | flops 3623878656 | bytes 14745600 | tf_op jit(solution)/shard_map/pallas_call | solution.py:40
  153.7 7.4 %shard_map.156.refs_14_.refs_15_ = f32[384,1024]{1,0:T(8,128)S(1)} custom-call(bf16[1024,7168]{1,0:T(8,128)(2,1)} %refs_0_.9, bf16[1024,7168]{1,0:T(8,128)(2,1)} %refs_1_.14, bf16[2,48,7168]{2,1,0:T(8,128)(2,1)S(1)} %copy-done, bf16[2,48,7168]{2,1,0:T(8,128)(2,1)S(1)} %collective-permute-done.9.refs_8_.refs_3_.refs_2_, ...), custom_call_target="tpu_custom_call" | custom-call | flops 3623878656 | bytes 14745600 | tf_op jit(solution)/shard_map/pallas_call | solution.py:40
  161.1 8.4 %shard_map.157 = (bf16[48,1024]{1,0:T(8,128)(2,1)S(1)}, bf16[48,1024]{1,0:T(8,128)(2,1)S(1)}, bf16[48,1024]{1,0:T(8,128)(2,1)S(1)}, bf16[48,1024]{1,0:T(8,128)(2...) custom-call(bf16[1024,7168]{1,0:T(8,128)(2,1)} %refs_0_.9, ...), custom_call_target="tpu_custom_call" | custom-call | flops 4026531840 | bytes 16384000 | tf_op jit(solution)/shard_map/pallas_call | solution.py:40
  177.1 3.8 %collective-permute-done.48.refs_7_ = bf16[48,1024]{1,0:T(8,128)(2,1)S(1)} collective-permute-done((bf16[48,1024]{1,0:T(8,128)(2,1)S(1)}, bf16[48,1024]{1,0:T(8,128)(2,1)S(1)}, u32[]{:S(2)}, u32[]{:S(2)}) %collective-permute-start.48) | collective-permute-done | bytes 98336 | tf_op jit(solution)/shard_map/ppermute | solution.py:383
  182.1 7.8 %shard_map.159 = (f32[7168,1024]{1,0:T(8,128)}, f32[8,128]{1,0:T(8,128)S(1)}) custom-call(bf16[8,48,1024]{2,1,0:T(8,128)(2,1)S(1)} %shard_map.136.refs_0_.refs_2_, bf16[2,48,7168]{2,1,0:T(8,128)(2,1)S(1)} %copy-done, bf16[2,48,7168]{2,1,0:T(8,128)(2,1)S(1)} %collective-permute-done.9.refs_8_.refs_3_.refs_2_, ...), custom_call_target="tpu_custom_call" | custom-call | flops 2818572288 | bytes 20185088 | tf_op jit(solution)/shard_map/pallas_call | solution.py:40
  189.9 3.8 %collective-permute-done.50.refs_1_ = bf16[4,48,1024]{2,1,0:T(8,128)(2,1)S(1)} collective-permute-done((bf16[4,48,1024]{2,1,0:T(8,128)(2,1)S(1)}, bf16[4,48,1024]{2,1,0:T(8,128)(2,1)S(1)}, u32[]{:S(2)}, u32[]{:S(2)}) %collective-permute-start.50) | collective-permute-done | bytes 393248 | tf_op jit(solution)/shard_map/ppermute | solution.py:377
  195.2 7.8 %shard_map.161 = (f32[7168,1024]{1,0:T(8,128)}, f32[8,128]{1,0:T(8,128)S(1)}) custom-call(bf16[8,48,1024]{2,1,0:T(8,128)(2,1)S(1)} %shard_map.136.refs_0_.refs_2_, bf16[2,48,7168]{2,1,0:T(8,128)(2,1)S(1)} %copy-done, bf16[2,48,7168]{2,1,0:T(8,128)(2,1)S(1)} %collective-permute-done.9.refs_8_.refs_3_.refs_2_, ...), custom_call_target="tpu_custom_call", output_to_operand_aliasing={{0}: (11, {})} | custom-call | flops 2818572288 | bytes 20185088 | tf_op jit(solution)/shard_map/pallas_call | solution.py:40
  206.0 3.8 %collective-permute-done.52.refs_1_ = f32[48,128]{1,0:T(8,128)S(1)} collective-permute-done((f32[48,128]{1,0:T(8,128)S(1)}, f32[48,128]{1,0:T(8,128)S(1)}, u32[]{:S(2)}, u32[]{:S(2)}) %collective-permute-start.52) | collective-permute-done | bytes 24608 | tf_op jit(solution)/shard_map/ppermute | solution.py:377
  210.7 3.8 %collective-permute-done.53.refs_6_ = f32[48,128]{1,0:T(8,128)S(1)} collective-permute-done((f32[48,128]{1,0:T(8,128)S(1)}, f32[48,128]{1,0:T(8,128)S(1)}, u32[]{:S(2)}, u32[]{:S(2)}) %collective-permute-start.53) | collective-permute-done | bytes 24608 | tf_op jit(solution)/shard_map/ppermute | solution.py:377
  (158 shorter events, 75.0 us)
Async XLA Ops:
  17.8 43.0 %collective-permute-start.9 = (bf16[2,48,7168]{2,1,0:T(8,128)(2,1)}, bf16[2,48,7168]{2,1,0:T(8,128)(2,1)S(1)}, u32[]{:S(2)}, u32[]{:S(2)}) collective-permute-start(bf16[2,48,7168]{2,1,0:T(8,128)(2,1)} %get-tuple-element.67.refs_2_.refs_1_), channel_id=1, source_target_pairs={{0,8},{4,20},{8,0},{12,28},{16,24},{20,4},{24,16},{28,12},{1,9},{5... | collective-permute-start | bytes 4128776 | tf_op jit(solution)/shard_map/ppermute | solution.py:374
  18.3 42.5 %collective-permute-start.10 = (bf16[1,48,7168]{2,1,0:T(8,128)(2,1)}, bf16[1,48,7168]{2,1,0:T(8,128)(2,1)S(1)}, u32[]{:S(2)}, u32[]{:S(2)}) collective-permute-start(bf16[1,48,7168]{2,1,0:T(8,128)(2,1)} %get-tuple-element.56.refs_13_), channel_id=1, source_target_pairs={{0,16},{4,12},{8,24},{12,4},{16,0},{20,28},{24,8},{28,20},{1,17},{... | collective-permute-start | bytes 2064392 | tf_op jit(solution)/shard_map/ppermute | solution.py:374
  18.6 9.9 %collective-permute-start.5 = (bf16[48,2048]{1,0:T(8,128)(2,1)}, bf16[48,2048]{1,0:T(8,128)(2,1)S(1)}, u32[]{:S(2)}, u32[]{:S(2)}) collective-permute-start(bf16[48,2048]{1,0:T(8,128)(2,1)} %refs_0_.11), channel_id=1, source_target_pairs={{0,3},{1,2},{2,1},{3,0},{4,7},{5,6},{6,5},{7,4},{8,11},{9,10},{10,... | collective-permute-start | bytes 589832 | tf_op jit(solution)/shard_map/ppermute | solution.py:377
  22.4 17.2 %collective-permute-start.4 = (bf16[48,2048]{1,0:T(8,128)(2,1)}, bf16[48,2048]{1,0:T(8,128)(2,1)S(1)}, u32[]{:S(2)}, u32[]{:S(2)}) collective-permute-start(bf16[48,2048]{1,0:T(8,128)(2,1)} %refs_0_.11), channel_id=1, source_target_pairs={{0,2},{1,3},{2,0},{3,1},{4,6},{5,7},{6,4},{7,5},{8,10},{9,11},{10,... | collective-permute-start | bytes 589832 | tf_op jit(solution)/shard_map/ppermute | solution.py:377
  22.5 17.2 %collective-permute-start.3 = (bf16[48,2048]{1,0:T(8,128)(2,1)}, bf16[48,2048]{1,0:T(8,128)(2,1)S(1)}, u32[]{:S(2)}, u32[]{:S(2)}) collective-permute-start(bf16[48,2048]{1,0:T(8,128)(2,1)} %refs_0_.11), channel_id=1, source_target_pairs={{0,1},{1,0},{2,3},{3,2},{4,5},{5,4},{6,7},{7,6},{8,9},{9,8},{10,11... | collective-permute-start | bytes 589832 | tf_op jit(solution)/shard_map/ppermute | solution.py:377
  62.7 18.3 %collective-permute-start.19 = (bf16[2,48,7168]{2,1,0:T(8,128)(2,1)S(1)}, bf16[2,48,7168]{2,1,0:T(8,128)(2,1)S(1)}, u32[]{:S(2)}, u32[]{:S(2)}) collective-permute-start(bf16[2,48,7168]{2,1,0:T(8,128)(2,1)S(1)} %collective-permute-done.9.refs_8_.refs_3_.refs_2_), channel_id=1, source_target_pairs={{0,16},{4,12},{8,24},{12,4},{16,0},{20,28},{24,8},{28,20},{1,17},{... | collective-permute-start | bytes 4128776 | tf_op jit(solution)/shard_map/ppermute | solution.py:374
  69.3 11.7 %collective-permute-start.25 = (bf16[4,48,2304]{2,1,0:T(8,128)(2,1)}, bf16[4,48,2304]{2,1,0:T(8,128)(2,1)S(1)}, u32[]{:S(2)}, u32[]{:S(2)}) collective-permute-start(bf16[4,48,2304]{2,1,0:T(8,128)(2,1)} %get-tuple-element.73.refs_5_), channel_id=1, source_target_pairs={{0,4},{4,0},{8,12},{12,8},{16,20},{20,16},{24,28},{28,24},{1,5},{5... | collective-permute-start | bytes 2654216 | tf_op jit(solution)/shard_map/ppermute | solution.py:370
  69.4 19.0 %collective-permute-start.18 = (bf16[1,48,7168]{2,1,0:T(8,128)(2,1)S(1)}, bf16[1,48,7168]{2,1,0:T(8,128)(2,1)S(1)}, u32[]{:S(2)}, u32[]{:S(2)}) collective-permute-start(bf16[1,48,7168]{2,1,0:T(8,128)(2,1)S(1)} %bitcast.15), channel_id=1, source_target_pairs={{0,16},{4,12},{8,24},{12,4},{16,0},{20,28},{24,8},{28,20},{1,17},{... | collective-permute-start | bytes 2064392 | tf_op jit(solution)/shard_map/ppermute | solution.py:374
  75.9 19.9 %collective-permute-start.28 = (bf16[4,48,2304]{2,1,0:T(8,128)(2,1)}, bf16[4,48,2304]{2,1,0:T(8,128)(2,1)}, u32[]{:S(2)}, u32[]{:S(2)}) collective-permute-start(bf16[4,48,2304]{2,1,0:T(8,128)(2,1)} %get-tuple-element.74.refs_2_), channel_id=1, source_target_pairs={{0,4},{4,0},{8,12},{12,8},{16,20},{20,16},{24,28},{28,24},{1,5},{5... | collective-permute-start | bytes 2654216 | tf_op jit(solution)/shard_map/ppermute | solution.py:370
  81.0 27.2 %collective-permute-start.24 = (bf16[2,48,7168]{2,1,0:T(8,128)(2,1)S(1)}, bf16[2,48,7168]{2,1,0:T(8,128)(2,1)S(1)}, u32[]{:S(2)}, u32[]{:S(2)}) collective-permute-start(bf16[2,48,7168]{2,1,0:T(8,128)(2,1)S(1)} %collective-permute-done.19.refs_3_.refs_6_.refs_5_), channel_id=1, source_target_pairs={{0,4},{4,0},{8,12},{12,8},{16,20},{20,16},{24,28},{28,24},{1,5},{5... | collective-permute-start | bytes 4128776 | tf_op jit(solution)/shard_map/ppermute | solution.py:370
  94.0 8.7 %collective-permute-start.26 = (bf16[4,48,2560]{2,1,0:T(8,128)(2,1)S(1)}, bf16[4,48,2560]{2,1,0:T(8,128)(2,1)S(1)}, u32[]{:S(2)}, u32[]{:S(2)}) collective-permute-start(bf16[4,48,2560]{2,1,0:T(8,128)(2,1)S(1)} %get-tuple-element.77.refs_2_), channel_id=1, source_target_pairs={{0,4},{4,0},{8,12},{12,8},{16,20},{20,16},{24,28},{28,24},{1,5},{5... | collective-permute-start | bytes 2949128 | tf_op jit(solution)/shard_map/ppermute | solution.py:370
  95.8 22.5 %collective-permute-start.23 = (bf16[1,48,7168]{2,1,0:T(8,128)(2,1)S(1)}, bf16[1,48,7168]{2,1,0:T(8,128)(2,1)S(1)}, u32[]{:S(2)}, u32[]{:S(2)}) collective-permute-start(bf16[1,48,7168]{2,1,0:T(8,128)(2,1)S(1)} %collective-permute-done.18.refs_2_.refs_5_.refs_4_), channel_id=1, source_target_pairs={{0,4},{4,0},{8,12},{12,8},{16,20},{20,16},{24,28},{28,24},{1,5},{5... | collective-permute-start | bytes 2064392 | tf_op jit(solution)/shard_map/ppermute | solution.py:370
  97.9 10.3 %collective-permute-start.31 = (bf16[2,48,2304]{2,1,0:T(8,128)(2,1)S(1)}, bf16[2,48,2304]{2,1,0:T(8,128)(2,1)S(1)}, u32[]{:S(2)}, u32[]{:S(2)}) collective-permute-start(bf16[2,48,2304]{2,1,0:T(8,128)(2,1)S(1)} %get-tuple-element.80.refs_2_), channel_id=1, source_target_pairs={{0,8},{4,20},{8,0},{12,28},{16,24},{20,4},{24,16},{28,12},{1,9},{5... | collective-permute-start | bytes 1327112 | tf_op jit(solution)/shard_map/ppermute | solution.py:374
  103.3 13.9 %collective-permute-start.29 = (bf16[2,48,2560]{2,1,0:T(8,128)(2,1)S(1)}, bf16[2,48,2560]{2,1,0:T(8,128)(2,1)S(1)}, u32[]{:S(2)}, u32[]{:S(2)}) collective-permute-start(bf16[2,48,2560]{2,1,0:T(8,128)(2,1)S(1)} %get-tuple-element.83.refs_3_), channel_id=1, source_target_pairs={{0,8},{4,20},{8,0},{12,28},{16,24},{20,4},{24,16},{28,12},{1,9},{5... | collective-permute-start | bytes 1474568 | tf_op jit(solution)/shard_map/ppermute | solution.py:374
  108.5 9.6 %collective-permute-start.34 = (bf16[1,48,2304]{2,1,0:T(8,128)(2,1)S(1)}, bf16[1,48,2304]{2,1,0:T(8,128)(2,1)S(1)}, u32[]{:S(2)}, u32[]{:S(2)}) collective-permute-start(bf16[1,48,2304]{2,1,0:T(8,128)(2,1)S(1)} %get-tuple-element.86.refs_2_), channel_id=1, source_target_pairs={{0,16},{4,12},{8,24},{12,4},{16,0},{20,28},{24,8},{28,20},{1,17},{... | collective-permute-start | bytes 663560 | tf_op jit(solution)/shard_map/ppermute | solution.py:374
  119.8 13.8 %collective-permute-start.36 = (bf16[2,48,2304]{2,1,0:T(8,128)(2,1)S(1)}, bf16[2,48,2304]{2,1,0:T(8,128)(2,1)S(1)}, u32[]{:S(2)}, u32[]{:S(2)}) collective-permute-start(bf16[2,48,2304]{2,1,0:T(8,128)(2,1)S(1)} %shard_map.148.refs_2_.refs_0_), channel_id=1, source_target_pairs={{0,16},{4,12},{8,24},{12,4},{16,0},{20,28},{24,8},{28,20},{1,17},{... | collective-permute-start | bytes 1327112 | tf_op jit(solution)/shard_map/ppermute | solution.py:374
  120.7 12.4 %collective-permute-start.32 = (bf16[1,48,2560]{2,1,0:T(8,128)(2,1)S(1)}, bf16[1,48,2560]{2,1,0:T(8,128)(2,1)S(1)}, u32[]{:S(2)}, u32[]{:S(2)}) collective-permute-start(bf16[1,48,2560]{2,1,0:T(8,128)(2,1)S(1)} %get-tuple-element.88.refs_2_), channel_id=1, source_target_pairs={{0,16},{4,12},{8,24},{12,4},{16,0},{20,28},{24,8},{28,20},{1,17},{... | collective-permute-start | bytes 737288 | tf_op jit(solution)/shard_map/ppermute | solution.py:374
  121.9 11.5 %collective-permute-start.37 = (bf16[1,48,2304]{2,1,0:T(8,128)(2,1)S(1)}, bf16[1,48,2304]{2,1,0:T(8,128)(2,1)S(1)}, u32[]{:S(2)}, u32[]{:S(2)}) collective-permute-start(bf16[1,48,2304]{2,1,0:T(8,128)(2,1)S(1)} %shard_map.147.refs_3_.refs_0_), channel_id=1, source_target_pairs={{0,8},{4,20},{8,0},{12,28},{16,24},{20,4},{24,16},{28,12},{1,9},{5... | collective-permute-start | bytes 663560 | tf_op jit(solution)/shard_map/ppermute | solution.py:374
  133.8 11.7 %collective-permute-start.39 = (bf16[4,48,2304]{2,1,0:T(8,128)(2,1)S(1)}, bf16[4,48,2304]{2,1,0:T(8,128)(2,1)S(1)}, u32[]{:S(2)}, u32[]{:S(2)}) collective-permute-start(bf16[4,48,2304]{2,1,0:T(8,128)(2,1)S(1)} %shard_map.151.refs_2_.refs_12_), channel_id=1, source_target_pairs={{0,4},{4,0},{8,12},{12,8},{16,20},{20,16},{24,28},{28,24},{1,5},{5... | collective-permute-start | bytes 2654216 | tf_op jit(solution)/shard_map/ppermute | solution.py:370
  133.9 11.3 %collective-permute-start.40 = (bf16[2,48,2304]{2,1,0:T(8,128)(2,1)S(1)}, bf16[2,48,2304]{2,1,0:T(8,128)(2,1)S(1)}, u32[]{:S(2)}, u32[]{:S(2)}) collective-permute-start(bf16[2,48,2304]{2,1,0:T(8,128)(2,1)S(1)} %shard_map.150.refs_2_.refs_0_), channel_id=1, source_target_pairs={{0,16},{4,12},{8,24},{12,4},{16,0},{20,28},{24,8},{28,20},{1,17},{... | collective-permute-start | bytes 1327112 | tf_op jit(solution)/shard_map/ppermute | solution.py:374
  134.8 8.9 %collective-permute-start.35 = (bf16[1,48,2560]{2,1,0:T(8,128)(2,1)S(1)}, bf16[1,48,2560]{2,1,0:T(8,128)(2,1)S(1)}, u32[]{:S(2)}, u32[]{:S(2)}) collective-permute-start(bf16[1,48,2560]{2,1,0:T(8,128)(2,1)S(1)} %shard_map.149.refs_2_.refs_0_), channel_id=1, source_target_pairs={{0,8},{4,20},{8,0},{12,28},{16,24},{20,4},{24,16},{28,12},{1,9},{5... | collective-permute-start | bytes 737288 | tf_op jit(solution)/shard_map/ppermute | solution.py:374
  143.9 8.9 %collective-permute-start.38 = (bf16[2,48,2560]{2,1,0:T(8,128)(2,1)S(1)}, bf16[2,48,2560]{2,1,0:T(8,128)(2,1)S(1)}, u32[]{:S(2)}, u32[]{:S(2)}) collective-permute-start(bf16[2,48,2560]{2,1,0:T(8,128)(2,1)S(1)} %shard_map.152.refs_2_.refs_0_), channel_id=1, source_target_pairs={{0,16},{4,12},{8,24},{12,4},{16,0},{20,28},{24,8},{28,20},{1,17},{... | collective-permute-start | bytes 1474568 | tf_op jit(solution)/shard_map/ppermute | solution.py:374
  182.0 11.7 %collective-permute-start.50 = (bf16[4,48,1024]{2,1,0:T(8,128)(2,1)S(1)}, bf16[4,48,1024]{2,1,0:T(8,128)(2,1)S(1)}, u32[]{:S(2)}, u32[]{:S(2)}) collective-permute-start(bf16[4,48,1024]{2,1,0:T(8,128)(2,1)S(1)} %get-tuple-element.99.refs_11_), channel_id=1, source_target_pairs={{0,1},{1,0},{2,3},{3,2},{4,5},{5,4},{6,7},{7,6},{8,9},{9,8},{10,11... | collective-permute-start | bytes 1179656 | tf_op jit(solution)/shard_map/ppermute | solution.py:377
  193.9 11.8 %collective-permute-start.51 = (bf16[2,48,1024]{2,1,0:T(8,128)(2,1)S(1)}, bf16[2,48,1024]{2,1,0:T(8,128)(2,1)S(1)}, u32[]{:S(2)}, u32[]{:S(2)}) collective-permute-start(bf16[2,48,1024]{2,1,0:T(8,128)(2,1)S(1)} %get-tuple-element.102.refs_12_), channel_id=1, source_target_pairs={{0,2},{1,3},{2,0},{3,1},{4,6},{5,7},{6,4},{7,5},{8,10},{9,11},{10,... | collective-permute-start | bytes 589832 | tf_op jit(solution)/shard_map/ppermute | solution.py:377
  (49 other events, 253.3 us)
where the time goes:
time: 218 us; the launch traced here: 215 us
  waiting for transfers between devices  91 us (42%)
  Pallas kernels  68.2 us (31%)
  starting transfers between devices  44.8 us (21%)
  local copies, waits for them, and re-layouts  10.3 us (5%)
    pallas_call x35, Pallas kernels, call(): pl.pallas_call(body, grid=grid, in_specs=list(ins) + [pl.BlockSpec(memory...  68.2 us
    ppermute x16, waiting for transfers between devices, linked(): return lax.ppermute(values, 'row', pairs)  44.3 us
    ppermute x10, waiting for transfers between devices, along(): return lax.ppermute(values, 'col', [(c, c ^ bit) for c in range(cols)])  30.6 us
    ppermute x16, starting transfers between devices, linked(): return lax.ppermute(values, 'row', pairs)  15.9 us
    ppermute x14, starting transfers between devices, exchanged(): lax.ppermute(tiles[q], 'row', pairs)  13.3 us
    ppermute x14, waiting for transfers between devices, exchanged(): lax.ppermute(tiles[q], 'row', pairs)  12.9 us
    ppermute x10, starting transfers between devices, along(): return lax.ppermute(values, 'col', [(c, c ^ bit) for c in range(cols)])  11.2 us
    unnamed x38, local copies, waits for them, and re-layouts  10.3 us
  transfers between devices with their start and end apart: 54, of which 26 were waited for; matrix products, arithmetic and copies ran while one was open for 0% of the time, Pallas kernels for 25%

commit v1 on v0

--- a/solution.py
+++ b/solution.py
@@ -98,10 +98,8 @@
     return label(place_ref, relative(place_ref, k, d) + own, links)
 
 
-def head_kernel(gain_ref, weight_ref, live_ref, head_ref, count_ref):
+def head_kernel(gain_ref, weight_ref, head_ref):
     head_ref[...] = gain_ref[...] * weight_ref[...]
-    count = jnp.sum(live_ref[...].astype(F32), axis=1, keepdims=True)
-    count_ref[...] = jnp.broadcast_to(count, count_ref.shape)
 
 
 def turn(values):
@@ -114,7 +112,7 @@
     return (root * (head * dvalue - rows_of * root * product)).astype(BF16)
 
 
-def out_kernel(tokens, k, links, place_ref, returns_ref, live_ref, count_ref, came_ref, *refs):
+def out_kernel(tokens, k, links, place_ref, returns_ref, live_ref, *refs):
     columns = (len(refs) - 2) // (2 + k)
     pieces, heads, outs = refs[:columns], refs[columns : 2 * columns], refs[2 * columns : -2]
     token_ref, held_ref = refs[-2:]
@@ -129,7 +127,8 @@
     rows = [returns_ref[...], live_ref[...].astype(F32)]
     rows = [jnp.concatenate([row, pad], axis=1) for row in rows] + [jnp.zeros((6, LANES), F32)]
     rows = turn(jnp.concatenate(rows, axis=0))[0:own]
-    factor = (tokens * math.sqrt(width)) / (count_ref[0:1, 0:1] + came_ref[0:1, 0:1])
+    factor = tokens * math.sqrt(width)
+    count = jnp.sum(column(rows, 1), axis=0, keepdims=True)
     root = lax.rsqrt(squares / width + epsilon)
     value = root * products
     dvalue = column(rows, 1) * (value - column(rows, 0)) * factor
@@ -142,7 +141,18 @@
                 pieces[d][:, part].astype(F32), token, heads[d][:, part]
             )
     for q, out in enumerate(outs):
-        out[...] = held_ref[q]
+        out[0:own, :] = held_ref[q]
+        out[own:, :] = jnp.broadcast_to(count, (out.shape[0] - own, tile)).astype(BF16)
+
+
+def gather_kernel(*refs):
+    tiles, (out_ref, inverse_ref) = refs[:-2], refs[-2:]
+    own = out_ref.shape[1]
+    count = 0.0
+    for q, ref in enumerate(tiles):
+        out_ref[q] = ref[0:own, :]
+        count = count + ref[own : own + 16, 0:LANES].astype(F32)
+    inverse_ref[...] = 1.0 / count[0:8]
 
 
 def arrange_kernel(k, links, place_ref, *refs):
@@ -244,7 +254,7 @@
     )
 
 
-def weight_kernel(links, picks, held, d_out_ref, *refs):
+def weight_kernel(links, picks, held, inverse_ref, d_out_ref, *refs):
     out_ref, done_ref = refs[-2:]
     mine, other = refs[:held], refs[held : 2 * held]
     count, own, tile = d_out_ref.shape
@@ -253,7 +263,7 @@
         for pair, position in ((mine, 2 * j), (other, other_core(j, links))):
             gate, up = (pair[i][at].astype(F32) for i, at in picks[j])
             hidden[position] = (gate * jax.nn.sigmoid(gate) * up).astype(BF16)
-    out_ref[...] = lax.dot_general(
+    out_ref[...] = inverse_ref[0:1, 0:1] * lax.dot_general(
         jnp.concatenate(hidden, axis=0),
         d_out_ref[...].reshape(count * own, tile),
         (((0,), (0,)), ((), ())),
@@ -262,7 +272,7 @@
     done_ref[...] = jnp.zeros_like(done_ref)
 
 
-def normed_kernel(links, picks, held, first, last, w_gate_ref, w_up_ref, *refs):
+def normed_kernel(links, picks, held, first, last, inverse_ref, w_gate_ref, w_up_ref, *refs):
     total = refs[-1]
     outs = refs[2 * held + (2 if first else 3) : -1]
     mine, other = refs[:held], refs[held : 2 * held]
@@ -279,7 +289,7 @@
         ):
             gate, up = (pair[i][at].astype(F32) for i, at in picks[j])
             sig = jax.nn.sigmoid(gate)
-            through = grad[j].astype(F32) * sig
+            through = grad[j].astype(F32) * inverse_ref[0:1, 0:1] * sig
             d_gates[position] = (through * up * (1.0 + gate * (1.0 - sig))).astype(BF16)
             d_ups[position] = (through * gate).astype(BF16)
     contracted = (((1,), (1,)), ((), ()))
@@ -324,15 +334,17 @@
 
 
 def result_kernel(
-    width, block_ref, mid_ref, head_ref, gain_ref, token_ref, sums_ref, came_ref, back_ref, out_ref
+    width, block_ref, mid_ref, head_ref, gain_ref, inverse_ref, token_ref, sums_ref, came_ref, back_ref, out_ref
 ):
     k, own, tile = back_ref.shape
     sums = sums_ref[...] + came_ref[...]
     root = lax.rsqrt(column(sums, 1) / width + epsilon)
     product = column(sums, 0) * root / width
+    inverse = inverse_ref[0:1, 0:1]
+    token = place([column(token_ref, 0), column(token_ref, 1) * inverse, column(token_ref, 2) * inverse], own)
     for s in range(k):
         part = slice(s * tile, (s + 1) * tile)
-        own_d_out = gradient_rows(block_ref[:, part].astype(F32), token_ref[...], head_ref[:, part])
+        own_d_out = gradient_rows(block_ref[:, part].astype(F32), token, head_ref[:, part])
         scaled = back_ref[s].astype(F32) * gain_ref[:, part]
         normalized = mid_ref[:, part].astype(F32) * root
         out_ref[:, part] = (own_d_out.astype(F32) + root * (scaled - normalized * product)).astype(BF16)
@@ -384,46 +396,45 @@
         return [came[q] for q in range(rows)]
 
     line = jax.ShapeDtypeStruct((8, LANES), F32)
-    mask = response_mask[None, :]
-    head, tally = call(
+    head = call(
         head_kernel,
         (1,),
-        [whole((1, block)), whole((1, block)), whole((1, own))],
-        [whole((1, block)), whole((8, LANES))],
-        [jax.ShapeDtypeStruct((1, block), F32), line],
-        [final_gain, value_weight, mask],
+        [whole((1, block)), whole((1, block))],
+        whole((1, block)),
+        jax.ShapeDtypeStruct((1, block), F32),
+        [final_gain, value_weight],
         cost=cost(block, block * 12),
+        limit=60,
     )
     heads = [head] + [along(head, d) for d in range(1, cols)]
     pieces = [block_out] + [along(block_out, d) for d in range(1, cols)]
-    for bit in link_bits:
-        tally = call(
-            pair_kernel,
-            (1,),
-            [whole((8, LANES))] * 2,
-            whole((8, LANES)),
-            line,
-            [tally, across(tally, bit)],
-            cost=cost(8 * LANES, 8 * LANES * 12),
-        )
-
-    paired, gate_own = stack([gate_pre, up_pre], own, [2, 1], after=heads[1:], limit=60)
+
+    paired, gate_own = stack([gate_pre, up_pre], own, [2, 1], after=heads[1:])
     hop_a = linked(paired, 0)
     gate_b = linked(gate_own, 1)
 
     *tiles, token = call(
         functools.partial(out_kernel, own * rows, k, links),
         (1,),
-        [smem, whole((1, own)), whole((1, own)), whole((8, LANES)), whole((8, LANES))]
+        [smem, whole((1, own)), whole((1, own))]
         + [whole((own, block))] * cols
         + [whole((1, block))] * cols,
-        [whole((own, tile))] * rows + [whole((own, LANES))],
-        [jax.ShapeDtypeStruct((own, tile), BF16)] * rows + [jax.ShapeDtypeStruct((own, LANES), F32)],
-        [where, returns[None, :], mask, tally, across(tally, 1), *pieces, *heads],
+        [whole((own + 16, tile))] * rows + [whole((own, LANES))],
+        [jax.ShapeDtypeStruct((own + 16, tile), BF16)] * rows + [jax.ShapeDtypeStruct((own, LANES), F32)],
+        [where, returns[None, :], response_mask[None, :], *pieces, *heads],
         scratch=[pltpu.VMEM((rows, own, tile), BF16)],
         cost=cost(own * width * 10, own * width * 4),
     )
-    (d_out,) = stack(exchanged(tiles), own, [rows], after=[hop_a, gate_b])
+    d_out, inverse = call(
+        gather_kernel,
+        (1,),
+        [whole((own + 16, tile))] * rows,
+        [whole((rows, own, tile)), whole((8, LANES))],
+        [jax.ShapeDtypeStruct((rows, own, tile), BF16), line],
+        exchanged(tiles),
+        cost=cost(0, rows * own * tile * 4),
+        after=[hop_a, gate_b],
+    )
 
     paired, hop_a, gate_b, up_late, d_out = lax.optimization_barrier(
         (paired, hop_a, gate_b, up_pre[None], d_out)
@@ -479,14 +490,14 @@
         fb = block_of(math.gcd(start, extent), 1024)
         weights = pl.BlockSpec((tile, fb), lambda i, f=start // fb: (0, f + i))
         ins = (
-            [weights, weights]
+            [whole((8, LANES)), weights, weights]
             + [
                 pl.BlockSpec((values.shape[0], own, fb), lambda i, f=start // fb: (0, 0, f + i))
                 for values in held + others
             ]
             + [pl.BlockSpec((count, own, fb), lambda i: (0, 0, i))] * 2
         )
-        args = [w_gate, w_up, *held, *others, *grads[number]]
+        args = [inverse, w_gate, w_up, *held, *others, *grads[number]]
         if not first:
             ins.append(whole((rows * own, tile)))
             args.append(total)
@@ -510,7 +521,7 @@
 
     waits = {
         (1, 0): others[:3],
-        (2, 0): held[3:5],
+        (1, 1): held[3:5],
         (1, links): others[4:5],
         (0, links + 2): others[3:4],
     }
@@ -519,7 +530,7 @@
     stages = 2 * links + 2
     for t in range(stages + len(chunks)):
         at = {number: t - number for number in range(len(chunks)) if 0 <= t - number <= stages}
-        for number in sorted(at, key=lambda number: (at[number] == stages, -number)):
+        for number in sorted(at, key=lambda number: ((at[number] == stages) == (t > stages), -number)):
             if at[number] < stages:
                 next(chains[number])
             else:
@@ -543,11 +554,11 @@
     for at, bit in enumerate(col_bits):
         received = along(send, bit)
         if at < 2:
-            ins = [whole((rows, own, tile))] + [
+            ins = [whole((8, LANES)), whole((rows, own, tile))] + [
                 pl.BlockSpec((values.shape[0], own, fb), lambda i, at=at: (0, 0, at * blocks + i))
                 for values in held + others
             ]
-            args = [d_out, *held, *others]
+            args = [inverse, d_out, *held, *others]
             aliases = {}
             if at:
                 ins.append(pl.BlockSpec(memory_space=pl.ANY))
@@ -597,10 +608,10 @@
     gradient = call(
         functools.partial(result_kernel, width),
         (1,),
-        [row_spec, row_spec, gain_spec, gain_spec] + [sums_spec] * 3 + [back_spec],
+        [row_spec, row_spec, gain_spec, gain_spec, whole((8, LANES))] + [sums_spec] * 3 + [back_spec],
         row_spec,
         jax.ShapeDtypeStruct((own, block), BF16),
-        [block_out, stream_mid, head, mlp_gain, token, sums, along(sums, col_bits[-1]), total],
+        [block_out, stream_mid, head, mlp_gain, inverse, token, sums, along(sums, col_bits[-1]), total],
         cost=cost(own * block * 14, own * block * 8),
     )
     return (gradient, d_w_down)

time: 218 us -> 219 us (level)
  waiting for transfers between devices: 91 us -> 97.7 us
  local copies, waits for them, and re-layouts: 10.3 us -> 5.85 us
    ppermute x16, waiting for transfers between devices: 44.3 us -> 48.8 us  [linked(): return lax.ppermute(values, 'row', pairs)]
    unnamed x38 -> x24, local copies, waits for them, and re-layouts: 10.3 us -> 5.85 us
    ppermute x14, waiting for transfers between devices: 12.9 us -> 16 us  [exchanged(): lax.ppermute(tiles[q], 'row', pairs)]
    ppermute x14 -> x11, starting transfers between devices: 4.41 us -> 2.18 us  [across(): return lax.ppermute(values, 'row', [(r, r ^ bit) for r in range(rows)])]
    pallas_call x35 -> x33, Pallas kernels: 68.2 us -> 67.5 us  [call(): pl.pallas_call(body, grid=grid, in_specs=list(ins) + [pl.BlockSpec(memory...]
  transfers between devices with their start and end apart: 54 -> 51, of which waited for: 26 -> 27; matrix products, arithmetic and copies ran while one was open for 0% -> 0% of each run, Pallas kernels for 25% -> 25%
where the time goes in v1:
time: 219 us; the launch traced here: 216 us
  waiting for transfers between devices  97.7 us (45%)
  Pallas kernels  67.5 us (31%)
  starting transfers between devices  43.4 us (20%)
  local copies, waits for them, and re-layouts  5.85 us (3%)
    pallas_call x33, Pallas kernels, call(): pl.pallas_call(body, grid=grid, in_specs=list(ins) + [pl.BlockSpec(memory...  67.5 us
    ppermute x16, waiting for transfers between devices, linked(): return lax.ppermute(values, 'row', pairs)  48.8 us
    ppermute x10, waiting for transfers between devices, along(): return lax.ppermute(values, 'col', [(c, c ^ bit) for c in range(cols)])  29.6 us
    ppermute x16, starting transfers between devices, linked(): return lax.ppermute(values, 'row', pairs)  16.3 us
    ppermute x14, waiting for transfers between devices, exchanged(): lax.ppermute(tiles[q], 'row', pairs)  16 us
    ppermute x14, starting transfers between devices, exchanged(): lax.ppermute(tiles[q], 'row', pairs)  13.3 us
    ppermute x10, starting transfers between devices, along(): return lax.ppermute(values, 'col', [(c, c ^ bit) for c in range(cols)])  11.7 us
    unnamed x24, local copies, waits for them, and re-layouts  5.85 us
  transfers between devices with their start and end apart: 51, of which 27 were waited for; matrix products, arithmetic and copies ran while one was open for 0% of the time, Pallas kernels for 25%

profile of v1, /device:TPU:4, one launch (start us, length us, event | category | flops | bytes accessed | tf_op | source)
XLA Modules:
  0.0 215.6 jit_solution(10329453960484424070)
XLA Ops:
  1.9 3.6 %collective-permute-start.5 = (f32[1,2048]{1,0:T(1,128)}, f32[1,2048]{1,0:T(1,128)S(1)}, u32[]{:S(2)}, u32[]{:S(2)}) collective-permute-start(f32[1,2048]{1,0:T(1,128)} %shard_map.131.refs_5_.refs_7_.refs_2_), channel_id=1, source_target_pairs={{0,3},{1,2},{2,1},{3,0},{4,7},{5,6},{6,5},{7,4},{8,11},{9,10},{10,... | collective-permute-start | bytes 24584 | tf_op jit(solution)/shard_map/ppermute | solution.py:389
  7.6 2.7 %collective-permute-done.4.refs_3_.refs_9_ = f32[1,2048]{1,0:T(1,128)S(1)} collective-permute-done((f32[1,2048]{1,0:T(1,128)}, f32[1,2048]{1,0:T(1,128)S(1)}, u32[]{:S(2)}, u32[]{:S(2)}) %collective-permute-start.4) | collective-permute-done | bytes 8224 | tf_op jit(solution)/shard_map/ppermute | solution.py:389
  21.3 5.5 %collective-permute-done.2.refs_6_ = bf16[48,2048]{1,0:T(8,128)(2,1)} collective-permute-done((bf16[48,2048]{1,0:T(8,128)(2,1)}, bf16[48,2048]{1,0:T(8,128)(2,1)}, u32[]{:S(2)}, u32[]{:S(2)}) %collective-permute-start.2) | collective-permute-done | bytes 196640 | tf_op jit(solution)/shard_map/ppermute | solution.py:389
  26.8 7.7 %collective-permute-done.1.refs_5_ = bf16[48,2048]{1,0:T(8,128)(2,1)} collective-permute-done((bf16[48,2048]{1,0:T(8,128)(2,1)}, bf16[48,2048]{1,0:T(8,128)(2,1)}, u32[]{:S(2)}, u32[]{:S(2)}) %collective-permute-start.1) | collective-permute-done | bytes 196640 | tf_op jit(solution)/shard_map/ppermute | solution.py:389
  43.0 3.1 %collective-permute-done.7.refs_2_ = bf16[64,1024]{1,0:T(8,128)(2,1)S(1)} collective-permute-done((bf16[64,1024]{1,0:T(8,128)(2,1)S(1)}, bf16[64,1024]{1,0:T(8,128)(2,1)S(1)}, u32[]{:S(2)}, u32[]{:S(2)}) %collective-permute-start.7) | collective-permute-done | bytes 131104 | tf_op jit(solution)/shard_map/ppermute | solution.py:395
  52.8 3.4 %collective-permute-done.12.refs_7_ = bf16[64,1024]{1,0:T(8,128)(2,1)S(1)} collective-permute-done((bf16[64,1024]{1,0:T(8,128)(2,1)S(1)}, bf16[64,1024]{1,0:T(8,128)(2,1)S(1)}, u32[]{:S(2)}, u32[]{:S(2)}) %collective-permute-start.12) | collective-permute-done | bytes 131104 | tf_op jit(solution)/shard_map/ppermute | solution.py:395
  58.3 5.3 %shard_map.135 = (bf16[4,48,2304]{2,1,0:T(8,128)(2,1)S(1)}, bf16[4,48,2304]{2,1,0:T(8,128)(2,1)}) custom-call(bf16[8,48,1024]{2,1,0:T(8,128)(2,1)S(1)} %get-tuple-element.71.refs_0_.refs_1_, bf16[7168,1024]{1,0:T(8,128)(2,1)} %refs_1_.11, f32[8,128]{1,0:T(8,128)S(1)} %get-tuple-element.65.refs_2_.refs_0_.refs_4_), custom_call_target="tpu_custom_call" | custom-call | flops 1811939328 | bytes 6488064 | tf_op jit(solution)/shard_map/pallas_call | solution.py:40
  66.8 4.5 %shard_map.136 = (bf16[4,48,2304]{2,1,0:T(8,128)(2,1)S(1)}, bf16[4,48,2304]{2,1,0:T(8,128)(2,1)S(1)}) custom-call(bf16[8,48,1024]{2,1,0:T(8,128)(2,1)S(1)} %get-tuple-element.71.refs_0_.refs_1_, bf16[7168,1024]{1,0:T(8,128)(2,1)} %refs_1_.11, bf16[2,48,7168]{2,1,0:T(8,128)(2,1)S(1)} %collective-permute-done.17.refs_2_.refs_8_.refs_7_, ...), custom_call_target="tpu_custom_call" | custom-call | flops 1811939328 | bytes 6488064 | tf_op jit(solution)/shard_map/pallas_call | solution.py:40
  71.6 3.5 %collective-permute-done.16.refs_3_.refs_7_.refs_6_ = bf16[2,48,7168]{2,1,0:T(8,128)(2,1)S(1)} collective-permute-done((bf16[2,48,7168]{2,1,0:T(8,128)(2,1)S(1)}, bf16[2,48,7168]{2,1,0:T(8,128)(2,1)S(1)}, u32[]{:S(2)}, u32[]{:S(2)}) %collective-permute-start.16) | collective-permute-done | bytes 1376288 | tf_op jit(solution)/shard_map/ppermute | solution.py:386
  77.3 5.7 %shard_map.138 = (bf16[4,48,2560]{2,1,0:T(8,128)(2,1)S(1)}, bf16[4,48,2560]{2,1,0:T(8,128)(2,1)S(1)}) custom-call(bf16[8,48,1024]{2,1,0:T(8,128)(2,1)S(1)} %get-tuple-element.71.refs_0_.refs_1_, bf16[7168,1024]{1,0:T(8,128)(2,1)} %refs_1_.11, bf16[2,48,2304]{2,1,0:T(8,128)(2,1)S(1)} %get-tuple-element.75.refs_2_), custom_call_target="tpu_custom_call" | custom-call | flops 2013265920 | bytes 7208960 | tf_op jit(solution)/shard_map/pallas_call | solution.py:40
  85.1 13.9 %collective-permute-done.15.refs_2_.refs_6_.refs_5_ = bf16[1,48,7168]{2,1,0:T(8,128)(2,1)S(1)} collective-permute-done((bf16[1,48,7168]{2,1,0:T(8,128)(2,1)S(1)}, bf16[1,48,7168]{2,1,0:T(8,128)(2,1)S(1)}, u32[]{:S(2)}, u32[]{:S(2)}) %collective-permute-start.15) | collective-permute-done | bytes 688160 | tf_op jit(solution)/shard_map/ppermute | solution.py:386
  103.5 6.7 %collective-permute-done.28.refs_1_ = bf16[2,48,2304]{2,1,0:T(8,128)(2,1)S(1)} collective-permute-done((bf16[2,48,2304]{2,1,0:T(8,128)(2,1)S(1)}, bf16[2,48,2304]{2,1,0:T(8,128)(2,1)S(1)}, u32[]{:S(2)}, u32[]{:S(2)}) %collective-permute-start.28) | collective-permute-done | bytes 442400 | tf_op jit(solution)/shard_map/ppermute | solution.py:386
  112.6 5.2 %collective-permute-done.26.refs_1_ = bf16[2,48,2560]{2,1,0:T(8,128)(2,1)S(1)} collective-permute-done((bf16[2,48,2560]{2,1,0:T(8,128)(2,1)S(1)}, bf16[2,48,2560]{2,1,0:T(8,128)(2,1)S(1)}, u32[]{:S(2)}, u32[]{:S(2)}) %collective-permute-start.26) | collective-permute-done | bytes 491552 | tf_op jit(solution)/shard_map/ppermute | solution.py:386
  123.6 10.1 %collective-permute-done.29.refs_1_ = bf16[1,48,2560]{2,1,0:T(8,128)(2,1)S(1)} collective-permute-done((bf16[1,48,2560]{2,1,0:T(8,128)(2,1)S(1)}, bf16[1,48,2560]{2,1,0:T(8,128)(2,1)S(1)}, u32[]{:S(2)}, u32[]{:S(2)}) %collective-permute-start.29) | collective-permute-done | bytes 245792 | tf_op jit(solution)/shard_map/ppermute | solution.py:386
  136.9 7.3 %shard_map.150.refs_2_.refs_15_ = f32[384,1024]{1,0:T(8,128)S(1)} custom-call(f32[8,128]{1,0:T(8,128)S(1)} %get-tuple-element.65.refs_2_.refs_0_.refs_4_, bf16[1024,7168]{1,0:T(8,128)(2,1)} %refs_1_.14, bf16[1024,7168]{1,0:T(8,128)(2,1)} %refs_2_.5, bf16[2,48,7168]{2,1,0:T(8,128)(2,1)S(1)} %get-tuple-element.67.refs_3_.refs_2_, ...), custom_call_target="tpu_custom_call" | custom-call | flops 3623878656 | bytes 14745600 | tf_op jit(solution)/shard_map/pallas_call | solution.py:40
  145.9 7.5 %collective-permute-done.36.refs_1_ = bf16[2,48,2560]{2,1,0:T(8,128)(2,1)S(1)} collective-permute-done((bf16[2,48,2560]{2,1,0:T(8,128)(2,1)S(1)}, bf16[2,48,2560]{2,1,0:T(8,128)(2,1)S(1)}, u32[]{:S(2)}, u32[]{:S(2)}) %collective-permute-start.36) | collective-permute-done | bytes 491552 | tf_op jit(solution)/shard_map/ppermute | solution.py:386
  153.8 7.5 %shard_map.154.refs_15_.refs_16_ = f32[384,1024]{1,0:T(8,128)S(1)} custom-call(f32[8,128]{1,0:T(8,128)S(1)} %get-tuple-element.65.refs_2_.refs_0_.refs_4_, bf16[1024,7168]{1,0:T(8,128)(2,1)} %refs_1_.14, bf16[1024,7168]{1,0:T(8,128)(2,1)} %refs_2_.5, bf16[2,48,7168]{2,1,0:T(8,128)(2,1)S(1)} %get-tuple-element.67.refs_3_.refs_2_, ...), custom_call_target="tpu_custom_call" | custom-call | flops 3623878656 | bytes 14745600 | tf_op jit(solution)/shard_map/pallas_call | solution.py:40
  161.2 8.4 %shard_map.155 = (bf16[48,1024]{1,0:T(8,128)(2,1)S(1)}, bf16[48,1024]{1,0:T(8,128)(2,1)S(1)}, bf16[48,1024]{1,0:T(8,128)(2,1)S(1)}, bf16[48,1024]{1,0:T(8,128)(2...) custom-call(f32[8,128]{1,0:T(8,128)S(1)} %get-tuple-element.65.refs_, ...), custom_call_target="tpu_custom_call" | custom-call | flops 4026531840 | bytes 16384000 | tf_op jit(solution)/shard_map/pallas_call | solution.py:40
  177.4 3.4 %collective-permute-done.45.refs_7_ = bf16[48,1024]{1,0:T(8,128)(2,1)S(1)} collective-permute-done((bf16[48,1024]{1,0:T(8,128)(2,1)S(1)}, bf16[48,1024]{1,0:T(8,128)(2,1)S(1)}, u32[]{:S(2)}, u32[]{:S(2)}) %collective-permute-start.45) | collective-permute-done | bytes 98336 | tf_op jit(solution)/shard_map/ppermute | solution.py:395
  183.2 7.8 %shard_map.157 = (f32[7168,1024]{1,0:T(8,128)}, f32[8,128]{1,0:T(8,128)S(1)}) custom-call(f32[8,128]{1,0:T(8,128)S(1)} %get-tuple-element.65.refs_2_.refs_0_.refs_4_, bf16[8,48,1024]{2,1,0:T(8,128)(2,1)S(1)} %get-tuple-element.71.refs_0_.refs_1_, bf16[2,48,7168]{2,1,0:T(8,128)(2,1)S(1)} %get-tuple-element.67.refs_3_.refs_2_, ...), custom_call_target="tpu_custom_call" | custom-call | flops 2818572288 | bytes 20185088 | tf_op jit(solution)/shard_map/pallas_call | solution.py:40
  191.0 3.3 %collective-permute-done.47.refs_1_ = bf16[4,48,1024]{2,1,0:T(8,128)(2,1)S(1)} collective-permute-done((bf16[4,48,1024]{2,1,0:T(8,128)(2,1)S(1)}, bf16[4,48,1024]{2,1,0:T(8,128)(2,1)S(1)}, u32[]{:S(2)}, u32[]{:S(2)}) %collective-permute-start.47) | collective-permute-done | bytes 393248 | tf_op jit(solution)/shard_map/ppermute | solution.py:389
  195.9 7.9 %shard_map.159 = (f32[7168,1024]{1,0:T(8,128)}, f32[8,128]{1,0:T(8,128)S(1)}) custom-call(f32[8,128]{1,0:T(8,128)S(1)} %get-tuple-element.65.refs_2_.refs_0_.refs_4_, bf16[8,48,1024]{2,1,0:T(8,128)(2,1)S(1)} %get-tuple-element.71.refs_0_.refs_1_, bf16[2,48,7168]{2,1,0:T(8,128)(2,1)S(1)} %get-tuple-element.67.refs_3_.refs_2_, ...), custom_call_target="tpu_custom_call", output_to_operand_aliasing={{0}: (12, {})} | custom-call | flops 2818572288 | bytes 20185088 | tf_op jit(solution)/shard_map/pallas_call | solution.py:40
  206.0 3.8 %collective-permute-done.49.refs_1_ = f32[48,128]{1,0:T(8,128)S(1)} collective-permute-done((f32[48,128]{1,0:T(8,128)S(1)}, f32[48,128]{1,0:T(8,128)S(1)}, u32[]{:S(2)}, u32[]{:S(2)}) %collective-permute-start.49) | collective-permute-done | bytes 24608 | tf_op jit(solution)/shard_map/ppermute | solution.py:389
  211.0 3.5 %collective-permute-done.50.refs_7_ = f32[48,128]{1,0:T(8,128)S(1)} collective-permute-done((f32[48,128]{1,0:T(8,128)S(1)}, f32[48,128]{1,0:T(8,128)S(1)}, u32[]{:S(2)}, u32[]{:S(2)}) %collective-permute-start.50) | collective-permute-done | bytes 24608 | tf_op jit(solution)/shard_map/ppermute | solution.py:389
  (136 shorter events, 73.3 us)
Async XLA Ops:
  14.8 41.4 %collective-permute-start.13 = (bf16[2,48,7168]{2,1,0:T(8,128)(2,1)S(1)}, bf16[2,48,7168]{2,1,0:T(8,128)(2,1)S(1)}, u32[]{:S(2)}, u32[]{:S(2)}) collective-permute-start(bf16[2,48,7168]{2,1,0:T(8,128)(2,1)S(1)} %get-tuple-element.67.refs_3_.refs_2_), channel_id=1, source_target_pairs={{0,8},{4,20},{8,0},{12,28},{16,24},{20,4},{24,16},{28,12},{1,9},{5... | collective-permute-start | bytes 4128776 | tf_op jit(solution)/shard_map/ppermute | solution.py:386
  16.3 39.9 %collective-permute-start.14 = (bf16[1,48,7168]{2,1,0:T(8,128)(2,1)}, bf16[1,48,7168]{2,1,0:T(8,128)(2,1)S(1)}, u32[]{:S(2)}, u32[]{:S(2)}) collective-permute-start(bf16[1,48,7168]{2,1,0:T(8,128)(2,1)} %get-tuple-element.54.refs_11_), channel_id=1, source_target_pairs={{0,16},{4,12},{8,24},{12,4},{16,0},{20,28},{24,8},{28,20},{1,17},{... | collective-permute-start | bytes 2064392 | tf_op jit(solution)/shard_map/ppermute | solution.py:386
  16.8 10.0 %collective-permute-start.2 = (bf16[48,2048]{1,0:T(8,128)(2,1)}, bf16[48,2048]{1,0:T(8,128)(2,1)}, u32[]{:S(2)}, u32[]{:S(2)}) collective-permute-start(bf16[48,2048]{1,0:T(8,128)(2,1)} %refs_0_.5), channel_id=1, source_target_pairs={{0,3},{1,2},{2,1},{3,0},{4,7},{5,6},{6,5},{7,4},{8,11},{9,10},{10,... | collective-permute-start | bytes 589832 | tf_op jit(solution)/shard_map/ppermute | solution.py:389
  18.3 16.2 %collective-permute-start.1 = (bf16[48,2048]{1,0:T(8,128)(2,1)}, bf16[48,2048]{1,0:T(8,128)(2,1)}, u32[]{:S(2)}, u32[]{:S(2)}) collective-permute-start(bf16[48,2048]{1,0:T(8,128)(2,1)} %refs_0_.5), channel_id=1, source_target_pairs={{0,2},{1,3},{2,0},{3,1},{4,6},{5,7},{6,4},{7,5},{8,10},{9,11},{10,... | collective-permute-start | bytes 589832 | tf_op jit(solution)/shard_map/ppermute | solution.py:389
  18.9 15.6 %collective-permute-start = (bf16[48,2048]{1,0:T(8,128)(2,1)}, bf16[48,2048]{1,0:T(8,128)(2,1)}, u32[]{:S(2)}, u32[]{:S(2)}) collective-permute-start(bf16[48,2048]{1,0:T(8,128)(2,1)} %refs_0_.5), channel_id=1, source_target_pairs={{0,1},{1,0},{2,3},{3,2},{4,5},{5,4},{6,7},{7,6},{8,9},{9,8},{10,11... | collective-permute-start | bytes 589832 | tf_op jit(solution)/shard_map/ppermute | solution.py:389
  56.3 10.5 %collective-permute-start.17 = (bf16[2,48,7168]{2,1,0:T(8,128)(2,1)S(1)}, bf16[2,48,7168]{2,1,0:T(8,128)(2,1)S(1)}, u32[]{:S(2)}, u32[]{:S(2)}) collective-permute-start(bf16[2,48,7168]{2,1,0:T(8,128)(2,1)S(1)} %get-tuple-element.67.refs_3_.refs_2_), channel_id=1, source_target_pairs={{0,4},{4,0},{8,12},{12,8},{16,20},{20,16},{24,28},{28,24},{1,5},{5... | collective-permute-start | bytes 4128776 | tf_op jit(solution)/shard_map/ppermute | solution.py:382
  56.3 10.4 %collective-permute-start.18 = (bf16[2,48,7168]{2,1,0:T(8,128)(2,1)S(1)}, bf16[2,48,7168]{2,1,0:T(8,128)(2,1)S(1)}, u32[]{:S(2)}, u32[]{:S(2)}) collective-permute-start(bf16[2,48,7168]{2,1,0:T(8,128)(2,1)S(1)} %collective-permute-done.13.refs_8_.refs_4_.refs_3_), channel_id=1, source_target_pairs={{0,4},{4,0},{8,12},{12,8},{16,20},{20,16},{24,28},{28,24},{1,5},{5... | collective-permute-start | bytes 4128776 | tf_op jit(solution)/shard_map/ppermute | solution.py:382
  56.8 18.3 %collective-permute-start.16 = (bf16[2,48,7168]{2,1,0:T(8,128)(2,1)S(1)}, bf16[2,48,7168]{2,1,0:T(8,128)(2,1)S(1)}, u32[]{:S(2)}, u32[]{:S(2)}) collective-permute-start(bf16[2,48,7168]{2,1,0:T(8,128)(2,1)S(1)} %collective-permute-done.13.refs_8_.refs_4_.refs_3_), channel_id=1, source_target_pairs={{0,16},{4,12},{8,24},{12,4},{16,0},{20,28},{24,8},{28,20},{1,17},{... | collective-permute-start | bytes 4128776 | tf_op jit(solution)/shard_map/ppermute | solution.py:386
  63.6 11.6 %collective-permute-start.22 = (bf16[4,48,2304]{2,1,0:T(8,128)(2,1)}, bf16[4,48,2304]{2,1,0:T(8,128)(2,1)}, u32[]{:S(2)}, u32[]{:S(2)}) collective-permute-start(bf16[4,48,2304]{2,1,0:T(8,128)(2,1)} %get-tuple-element.73.refs_5_), channel_id=1, source_target_pairs={{0,4},{4,0},{8,12},{12,8},{16,20},{20,16},{24,28},{28,24},{1,5},{5... | collective-permute-start | bytes 2654216 | tf_op jit(solution)/shard_map/ppermute | solution.py:382
  71.3 27.6 %collective-permute-start.25 = (bf16[4,48,2304]{2,1,0:T(8,128)(2,1)S(1)}, bf16[4,48,2304]{2,1,0:T(8,128)(2,1)S(1)}, u32[]{:S(2)}, u32[]{:S(2)}) collective-permute-start(bf16[4,48,2304]{2,1,0:T(8,128)(2,1)S(1)} %get-tuple-element.74.refs_2_), channel_id=1, source_target_pairs={{0,4},{4,0},{8,12},{12,8},{16,20},{20,16},{24,28},{28,24},{1,5},{5... | collective-permute-start | bytes 2654216 | tf_op jit(solution)/shard_map/ppermute | solution.py:382
  75.1 35.0 %collective-permute-start.21 = (bf16[2,48,7168]{2,1,0:T(8,128)(2,1)S(1)}, bf16[2,48,7168]{2,1,0:T(8,128)(2,1)S(1)}, u32[]{:S(2)}, u32[]{:S(2)}) collective-permute-start(bf16[2,48,7168]{2,1,0:T(8,128)(2,1)S(1)} %collective-permute-done.16.refs_3_.refs_7_.refs_6_), channel_id=1, source_target_pairs={{0,4},{4,0},{8,12},{12,8},{16,20},{20,16},{24,28},{28,24},{1,5},{5... | collective-permute-start | bytes 4128776 | tf_op jit(solution)/shard_map/ppermute | solution.py:382
  83.0 17.9 %collective-permute-start.23 = (bf16[4,48,2560]{2,1,0:T(8,128)(2,1)S(1)}, bf16[4,48,2560]{2,1,0:T(8,128)(2,1)S(1)}, u32[]{:S(2)}, u32[]{:S(2)}) collective-permute-start(bf16[4,48,2560]{2,1,0:T(8,128)(2,1)S(1)} %get-tuple-element.77.refs_4_), channel_id=1, source_target_pairs={{0,4},{4,0},{8,12},{12,8},{16,20},{20,16},{24,28},{28,24},{1,5},{5... | collective-permute-start | bytes 2949128 | tf_op jit(solution)/shard_map/ppermute | solution.py:382
  83.6 15.4 %collective-permute-start.15 = (bf16[1,48,7168]{2,1,0:T(8,128)(2,1)S(1)}, bf16[1,48,7168]{2,1,0:T(8,128)(2,1)S(1)}, u32[]{:S(2)}, u32[]{:S(2)}) collective-permute-start(bf16[1,48,7168]{2,1,0:T(8,128)(2,1)S(1)} %bitcast.8), channel_id=1, source_target_pairs={{0,16},{4,12},{8,24},{12,4},{16,0},{20,28},{24,8},{28,20},{1,17},{... | collective-permute-start | bytes 2064392 | tf_op jit(solution)/shard_map/ppermute | solution.py:386
  85.1 15.6 %collective-permute-start.24 = (bf16[2,48,2304]{2,1,0:T(8,128)(2,1)S(1)}, bf16[2,48,2304]{2,1,0:T(8,128)(2,1)S(1)}, u32[]{:S(2)}, u32[]{:S(2)}) collective-permute-start(bf16[2,48,2304]{2,1,0:T(8,128)(2,1)S(1)} %get-tuple-element.75.refs_2_), channel_id=1, source_target_pairs={{0,8},{4,20},{8,0},{12,28},{16,24},{20,4},{24,16},{28,12},{1,9},{5... | collective-permute-start | bytes 1327112 | tf_op jit(solution)/shard_map/ppermute | solution.py:386
  98.9 20.1 %collective-permute-start.20 = (bf16[1,48,7168]{2,1,0:T(8,128)(2,1)S(1)}, bf16[1,48,7168]{2,1,0:T(8,128)(2,1)S(1)}, u32[]{:S(2)}, u32[]{:S(2)}) collective-permute-start(bf16[1,48,7168]{2,1,0:T(8,128)(2,1)S(1)} %collective-permute-done.15.refs_2_.refs_6_.refs_5_), channel_id=1, source_target_pairs={{0,4},{4,0},{8,12},{12,8},{16,20},{20,16},{24,28},{28,24},{1,5},{5... | collective-permute-start | bytes 2064392 | tf_op jit(solution)/shard_map/ppermute | solution.py:382
  99.4 10.7 %collective-permute-start.28 = (bf16[2,48,2304]{2,1,0:T(8,128)(2,1)S(1)}, bf16[2,48,2304]{2,1,0:T(8,128)(2,1)S(1)}, u32[]{:S(2)}, u32[]{:S(2)}) collective-permute-start(bf16[2,48,2304]{2,1,0:T(8,128)(2,1)S(1)} %get-tuple-element.80.refs_2_), channel_id=1, source_target_pairs={{0,8},{4,20},{8,0},{12,28},{16,24},{20,4},{24,16},{28,12},{1,9},{5... | collective-permute-start | bytes 1327112 | tf_op jit(solution)/shard_map/ppermute | solution.py:386
  101.5 16.3 %collective-permute-start.26 = (bf16[2,48,2560]{2,1,0:T(8,128)(2,1)S(1)}, bf16[2,48,2560]{2,1,0:T(8,128)(2,1)S(1)}, u32[]{:S(2)}, u32[]{:S(2)}) collective-permute-start(bf16[2,48,2560]{2,1,0:T(8,128)(2,1)S(1)} %get-tuple-element.83.refs_3_), channel_id=1, source_target_pairs={{0,8},{4,20},{8,0},{12,28},{16,24},{20,4},{24,16},{28,12},{1,9},{5... | collective-permute-start | bytes 1474568 | tf_op jit(solution)/shard_map/ppermute | solution.py:386
  120.3 13.8 %collective-permute-start.33 = (bf16[2,48,2304]{2,1,0:T(8,128)(2,1)S(1)}, bf16[2,48,2304]{2,1,0:T(8,128)(2,1)S(1)}, u32[]{:S(2)}, u32[]{:S(2)}) collective-permute-start(bf16[2,48,2304]{2,1,0:T(8,128)(2,1)S(1)} %shard_map.146.refs_2_.refs_0_), channel_id=1, source_target_pairs={{0,16},{4,12},{8,24},{12,4},{16,0},{20,28},{24,8},{28,20},{1,17},{... | collective-permute-start | bytes 1327112 | tf_op jit(solution)/shard_map/ppermute | solution.py:386
  121.4 12.3 %collective-permute-start.29 = (bf16[1,48,2560]{2,1,0:T(8,128)(2,1)S(1)}, bf16[1,48,2560]{2,1,0:T(8,128)(2,1)S(1)}, u32[]{:S(2)}, u32[]{:S(2)}) collective-permute-start(bf16[1,48,2560]{2,1,0:T(8,128)(2,1)S(1)} %get-tuple-element.88.refs_2_), channel_id=1, source_target_pairs={{0,16},{4,12},{8,24},{12,4},{16,0},{20,28},{24,8},{28,20},{1,17},{... | collective-permute-start | bytes 737288 | tf_op jit(solution)/shard_map/ppermute | solution.py:386
  122.4 11.5 %collective-permute-start.34 = (bf16[1,48,2304]{2,1,0:T(8,128)(2,1)S(1)}, bf16[1,48,2304]{2,1,0:T(8,128)(2,1)S(1)}, u32[]{:S(2)}, u32[]{:S(2)}) collective-permute-start(bf16[1,48,2304]{2,1,0:T(8,128)(2,1)S(1)} %shard_map.145.refs_3_.refs_0_), channel_id=1, source_target_pairs={{0,8},{4,20},{8,0},{12,28},{16,24},{20,4},{24,16},{28,12},{1,9},{5... | collective-permute-start | bytes 663560 | tf_op jit(solution)/shard_map/ppermute | solution.py:386
  134.5 9.7 %collective-permute-start.32 = (bf16[1,48,2560]{2,1,0:T(8,128)(2,1)S(1)}, bf16[1,48,2560]{2,1,0:T(8,128)(2,1)S(1)}, u32[]{:S(2)}, u32[]{:S(2)}) collective-permute-start(bf16[1,48,2560]{2,1,0:T(8,128)(2,1)S(1)} %shard_map.147.refs_2_.refs_0_), channel_id=1, source_target_pairs={{0,8},{4,20},{8,0},{12,28},{16,24},{20,4},{24,16},{28,12},{1,9},{5... | collective-permute-start | bytes 737288 | tf_op jit(solution)/shard_map/ppermute | solution.py:386
  135.7 9.8 %collective-permute-start.37 = (bf16[2,48,2304]{2,1,0:T(8,128)(2,1)S(1)}, bf16[2,48,2304]{2,1,0:T(8,128)(2,1)S(1)}, u32[]{:S(2)}, u32[]{:S(2)}) collective-permute-start(bf16[2,48,2304]{2,1,0:T(8,128)(2,1)S(1)} %shard_map.148.refs_2_.refs_0_), channel_id=1, source_target_pairs={{0,16},{4,12},{8,24},{12,4},{16,0},{20,28},{24,8},{28,20},{1,17},{... | collective-permute-start | bytes 1327112 | tf_op jit(solution)/shard_map/ppermute | solution.py:386
  183.1 11.2 %collective-permute-start.47 = (bf16[4,48,1024]{2,1,0:T(8,128)(2,1)S(1)}, bf16[4,48,1024]{2,1,0:T(8,128)(2,1)S(1)}, u32[]{:S(2)}, u32[]{:S(2)}) collective-permute-start(bf16[4,48,1024]{2,1,0:T(8,128)(2,1)S(1)} %get-tuple-element.99.refs_12_), channel_id=1, source_target_pairs={{0,1},{1,0},{2,3},{3,2},{4,5},{5,4},{6,7},{7,6},{8,9},{9,8},{10,11... | collective-permute-start | bytes 1179656 | tf_op jit(solution)/shard_map/ppermute | solution.py:389
  194.4 11.3 %collective-permute-start.48 = (bf16[2,48,1024]{2,1,0:T(8,128)(2,1)S(1)}, bf16[2,48,1024]{2,1,0:T(8,128)(2,1)S(1)}, u32[]{:S(2)}, u32[]{:S(2)}) collective-permute-start(bf16[2,48,1024]{2,1,0:T(8,128)(2,1)S(1)} %get-tuple-element.102.refs_13_), channel_id=1, source_target_pairs={{0,2},{1,3},{2,0},{3,1},{4,6},{5,7},{6,4},{7,5},{8,10},{9,11},{10,... | collective-permute-start | bytes 589832 | tf_op jit(solution)/shard_map/ppermute | solution.py:389
  (39 other events, 226.5 us)

commit v2 on v1

--- a/solution.py
+++ b/solution.py
@@ -98,8 +98,15 @@
     return label(place_ref, relative(place_ref, k, d) + own, links)
 
 
-def head_kernel(gain_ref, weight_ref, head_ref):
-    head_ref[...] = gain_ref[...] * weight_ref[...]
+def pack_kernel(out_ref, gain_ref, weight_ref, packed_ref):
+    own, block = out_ref.shape
+    head = gain_ref[...] * weight_ref[...]
+    high = head.astype(BF16)
+    rest = head - high.astype(F32)
+    middle = rest.astype(BF16)
+    low = (rest - middle.astype(F32)).astype(BF16)
+    packed_ref[0:own, :] = out_ref[...]
+    packed_ref[own:, :] = jnp.concatenate([high, middle, low] + [jnp.zeros((1, block), BF16)] * 13, axis=0)
 
 
 def turn(values):
@@ -113,16 +120,19 @@
 
 
 def out_kernel(tokens, k, links, place_ref, returns_ref, live_ref, *refs):
-    columns = (len(refs) - 2) // (2 + k)
-    pieces, heads, outs = refs[:columns], refs[columns : 2 * columns], refs[2 * columns : -2]
-    token_ref, held_ref = refs[-2:]
-    own, block = pieces[0].shape
+    columns = (len(refs) - 2) // (1 + k)
+    pieces, outs, (token_ref, held_ref) = refs[:columns], refs[columns:-2], refs[-2:]
+    own, block = token_ref.shape[0], pieces[0].shape[1]
+    heads = []
+    for piece in pieces:
+        parts = piece[own : own + 16, :].astype(F32)
+        heads.append(parts[0:1] + parts[1:2] + parts[2:3])
     width, tile = block * columns, block // k
     squares = products = jnp.zeros((own, 1), F32)
     for piece, head in zip(pieces, heads):
-        wide = piece[...].astype(F32)
+        wide = piece[0:own, :].astype(F32)
         squares = squares + jnp.sum(wide * wide, axis=1, keepdims=True)
-        products = products + jnp.sum(wide * head[...], axis=1, keepdims=True)
+        products = products + jnp.sum(wide * head, axis=1, keepdims=True)
     pad = jnp.zeros((1, LANES - own), F32)
     rows = [returns_ref[...], live_ref[...].astype(F32)]
     rows = [jnp.concatenate([row, pad], axis=1) for row in rows] + [jnp.zeros((6, LANES), F32)]
@@ -138,7 +148,7 @@
         for s in range(k):
             part = slice(s * tile, (s + 1) * tile)
             held_ref[slot(place_ref, k, links, d, s)] = gradient_rows(
-                pieces[d][:, part].astype(F32), token, heads[d][:, part]
+                pieces[d][0:own, part].astype(F32), token, heads[d][:, part]
             )
     for q, out in enumerate(outs):
         out[0:own, :] = held_ref[q]
@@ -329,22 +339,21 @@
     sums_ref[...] = place([products, squares], own)
 
 
-def pair_kernel(first_ref, second_ref, out_ref):
-    out_ref[...] = first_ref[...] + second_ref[...]
-
-
 def result_kernel(
-    width, block_ref, mid_ref, head_ref, gain_ref, inverse_ref, token_ref, sums_ref, came_ref, back_ref, out_ref
+    width, block_ref, mid_ref, norm_ref, weight_ref, gain_ref, inverse_ref, token_ref, back_ref, *refs
 ):
+    sums_refs, out_ref = refs[:-1], refs[-1]
     k, own, tile = back_ref.shape
-    sums = sums_ref[...] + came_ref[...]
+    sums = functools.reduce(lambda a, b: a + b, [ref[...] for ref in sums_refs])
     root = lax.rsqrt(column(sums, 1) / width + epsilon)
     product = column(sums, 0) * root / width
     inverse = inverse_ref[0:1, 0:1]
     token = place([column(token_ref, 0), column(token_ref, 1) * inverse, column(token_ref, 2) * inverse], own)
     for s in range(k):
         part = slice(s * tile, (s + 1) * tile)
-        own_d_out = gradient_rows(block_ref[:, part].astype(F32), token, head_ref[:, part])
+        own_d_out = gradient_rows(
+            block_ref[:, part].astype(F32), token, norm_ref[:, part] * weight_ref[:, part]
+        )
         scaled = back_ref[s].astype(F32) * gain_ref[:, part]
         normalized = mid_ref[:, part].astype(F32) * root
         out_ref[:, part] = (own_d_out.astype(F32) + root * (scaled - normalized * product)).astype(BF16)
@@ -396,32 +405,30 @@
         return [came[q] for q in range(rows)]
 
     line = jax.ShapeDtypeStruct((8, LANES), F32)
-    head = call(
-        head_kernel,
+    packed = call(
+        pack_kernel,
         (1,),
-        [whole((1, block)), whole((1, block))],
-        whole((1, block)),
-        jax.ShapeDtypeStruct((1, block), F32),
-        [final_gain, value_weight],
-        cost=cost(block, block * 12),
+        [whole((own, block)), whole((1, block)), whole((1, block))],
+        whole((own + 16, block)),
+        jax.ShapeDtypeStruct((own + 16, block), BF16),
+        [block_out, final_gain, value_weight],
+        cost=cost(block, own * block * 4),
         limit=60,
     )
-    heads = [head] + [along(head, d) for d in range(1, cols)]
-    pieces = [block_out] + [along(block_out, d) for d in range(1, cols)]
-
-    paired, gate_own = stack([gate_pre, up_pre], own, [2, 1], after=heads[1:])
+    pieces = [packed] + [along(packed, d) for d in range(1, cols)]
+
+    (paired,) = stack([gate_pre, up_pre], own, [2])
     hop_a = linked(paired, 0)
-    gate_b = linked(gate_own, 1)
+    hop_b = linked(paired, 1)
 
     *tiles, token = call(
         functools.partial(out_kernel, own * rows, k, links),
         (1,),
         [smem, whole((1, own)), whole((1, own))]
-        + [whole((own, block))] * cols
-        + [whole((1, block))] * cols,
+        + [whole((own + 16, block))] * cols,
         [whole((own + 16, tile))] * rows + [whole((own, LANES))],
         [jax.ShapeDtypeStruct((own + 16, tile), BF16)] * rows + [jax.ShapeDtypeStruct((own, LANES), F32)],
-        [where, returns[None, :], response_mask[None, :], *pieces, *heads],
+        [where, returns[None, :], response_mask[None, :], *pieces],
         scratch=[pltpu.VMEM((rows, own, tile), BF16)],
         cost=cost(own * width * 10, own * width * 4),
     )
@@ -433,15 +440,12 @@
         [jax.ShapeDtypeStruct((rows, own, tile), BF16), line],
         exchanged(tiles),
         cost=cost(0, rows * own * tile * 4),
-        after=[hop_a, gate_b],
-    )
-
-    paired, hop_a, gate_b, up_late, d_out = lax.optimization_barrier(
-        (paired, hop_a, gate_b, up_pre[None], d_out)
-    )
-    up_b = linked(up_late, 1)
-    held = [paired, hop_a, gate_b, up_b, linked(hop_a, 1)]
-    picks = [((0, 0), (0, 1)), ((1, 0), (1, 1)), ((2, 0), (3, 0)), ((4, 0), (4, 1))]
+        after=[hop_a, hop_b],
+    )
+
+    paired, hop_a, hop_b, d_out = lax.optimization_barrier((paired, hop_a, hop_b, d_out))
+    held = [paired, hop_a, hop_b, linked(hop_a, 1)]
+    picks = [((i, 0), (i, 1)) for i in range(4)]
     for i in range(2, links):
         picks = picks + [tuple((at + len(held), j) for at, j in pair) for pair in picks]
         held = held + [linked(values, i) for values in held]
@@ -520,21 +524,22 @@
         return result if last else result[0]
 
     waits = {
-        (1, 0): others[:3],
-        (1, 1): held[3:5],
-        (1, links): others[4:5],
-        (0, links + 2): others[3:4],
+        (1, 0): others[:1],
+        (2, 0): others[1:3],
+        (0, links): held[3:4],
+        (0, links + 1): others[3:4],
     }
     grads, total = {}, None
     chains = [reduced(number) for number in range(len(chunks))]
-    stages = 2 * links + 2
-    for t in range(stages + len(chunks)):
-        at = {number: t - number for number in range(len(chunks)) if 0 <= t - number <= stages}
-        for number in sorted(at, key=lambda number: ((at[number] == stages) == (t > stages), -number)):
-            if at[number] < stages:
-                next(chains[number])
-            else:
-                total = normed(number, total)
+    for _ in range(2 * links + 1):
+        for chain in chains:
+            next(chain)
+    next(chains[0])
+    total = normed(0, total)
+    for chain in chains[1:]:
+        next(chain)
+    for number in range(1, len(chunks)):
+        total = normed(number, total)
 
     keep, send = call(
         functools.partial(arrange_kernel, k, links),
@@ -595,23 +600,14 @@
         [stream_mid, mlp_gain, total],
         cost=cost(own * block * 5, own * block * 4),
     )
-    for bit in col_bits[:-1]:
-        sums = call(
-            pair_kernel,
-            (1,),
-            [sums_spec] * 2,
-            sums_spec,
-            jax.ShapeDtypeStruct((own, LANES), F32),
-            [sums, along(sums, bit)],
-            cost=cost(own * LANES, own * LANES * 12),
-        )
     gradient = call(
         functools.partial(result_kernel, width),
         (1,),
-        [row_spec, row_spec, gain_spec, gain_spec, whole((8, LANES))] + [sums_spec] * 3 + [back_spec],
+        [row_spec, row_spec] + [gain_spec] * 3 + [whole((8, LANES)), sums_spec, back_spec] + [sums_spec] * cols,
         row_spec,
         jax.ShapeDtypeStruct((own, block), BF16),
-        [block_out, stream_mid, head, mlp_gain, inverse, token, sums, along(sums, col_bits[-1]), total],
+        [block_out, stream_mid, final_gain, value_weight, mlp_gain, inverse, token, total, sums]
+        + [along(sums, d) for d in range(1, cols)],
         cost=cost(own * block * 14, own * block * 8),
     )
     return (gradient, d_w_down)

time: 219 us -> 194 us (0.89)
  waiting for transfers between devices: 97.7 us -> 75.4 us
  local copies, waits for them, and re-layouts: 5.85 us -> 2.23 us
    ppermute x16 -> x15, waiting for transfers between devices: 48.8 us -> 32.6 us  [linked(): return lax.ppermute(values, 'row', pairs)]
    unnamed x24 -> x20, local copies, waits for them, and re-layouts: 5.85 us -> 2.23 us
    ppermute x10 -> x8, waiting for transfers between devices: 29.6 us -> 26.5 us  [along(): return lax.ppermute(values, 'col', [(c, c ^ bit) for c in range(cols)])]
    ppermute x16 -> x15, starting transfers between devices: 16.3 us -> 17.4 us  [linked(): return lax.ppermute(values, 'row', pairs)]
    ppermute x10 -> x8, starting transfers between devices: 11.7 us -> 12.7 us  [along(): return lax.ppermute(values, 'col', [(c, c ^ bit) for c in range(cols)])]
    pallas_call x33 -> x32, Pallas kernels: 67.5 us -> 67.8 us  [call(): pl.pallas_call(body, grid=grid, in_specs=list(ins) + [pl.BlockSpec(memory...]
  transfers between devices with their start and end apart: 51 -> 47, of which waited for: 27 -> 24; matrix products, arithmetic and copies ran while one was open for 0% -> 0% of each run, Pallas kernels for 25% -> 29%
where the time goes in v2:
time: 194 us; the launch traced here: 192 us
  waiting for transfers between devices  75.4 us (39%)
  Pallas kernels  67.8 us (35%)
  starting transfers between devices  45.2 us (23%)
  local copies, waits for them, and re-layouts  2.23 us (1%)
    pallas_call x32, Pallas kernels, call(): pl.pallas_call(body, grid=grid, in_specs=list(ins) + [pl.BlockSpec(memory...  67.8 us
    ppermute x15, waiting for transfers between devices, linked(): return lax.ppermute(values, 'row', pairs)  32.6 us
    ppermute x8, waiting for transfers between devices, along(): return lax.ppermute(values, 'col', [(c, c ^ bit) for c in range(cols)])  26.5 us
    ppermute x15, starting transfers between devices, linked(): return lax.ppermute(values, 'row', pairs)  17.4 us
    ppermute x14, waiting for transfers between devices, exchanged(): lax.ppermute(tiles[q], 'row', pairs)  15.3 us
    ppermute x14, starting transfers between devices, exchanged(): lax.ppermute(tiles[q], 'row', pairs)  13.5 us
    ppermute x8, starting transfers between devices, along(): return lax.ppermute(values, 'col', [(c, c ^ bit) for c in range(cols)])  12.7 us
  transfers between devices with their start and end apart: 47, of which 24 were waited for; matrix products, arithmetic and copies ran while one was open for 0% of the time, Pallas kernels for 29%

profile of v2, /device:TPU:4, one launch (start us, length us, event | category | flops | bytes accessed | tf_op | source)
XLA Modules:
  0.0 191.8 jit_solution(3885125321322790458)
XLA Ops:
  7.0 3.6 %collective-permute-start.2 = (bf16[64,2048]{1,0:T(8,128)(2,1)}, bf16[64,2048]{1,0:T(8,128)(2,1)S(1)}, u32[]{:S(2)}, u32[]{:S(2)}) collective-permute-start(bf16[64,2048]{1,0:T(8,128)(2,1)} %shard_map.131.refs_2_.refs_3_), channel_id=1, source_target_pairs={{0,3},{1,2},{2,1},{3,0},{4,7},{5,6},{6,5},{7,4},{8,11},{9,10},{10,... | collective-permute-start | bytes 786440 | tf_op jit(solution)/shard_map/ppermute | solution.py:398
  11.5 6.9 %collective-permute-done.2.refs_6_ = bf16[64,2048]{1,0:T(8,128)(2,1)S(1)} collective-permute-done((bf16[64,2048]{1,0:T(8,128)(2,1)}, bf16[64,2048]{1,0:T(8,128)(2,1)S(1)}, u32[]{:S(2)}, u32[]{:S(2)}) %collective-permute-start.2) | collective-permute-done | bytes 262176 | tf_op jit(solution)/shard_map/ppermute | solution.py:398
  18.4 14.2 %collective-permute-done.1.refs_5_ = bf16[64,2048]{1,0:T(8,128)(2,1)S(1)} collective-permute-done((bf16[64,2048]{1,0:T(8,128)(2,1)}, bf16[64,2048]{1,0:T(8,128)(2,1)S(1)}, u32[]{:S(2)}, u32[]{:S(2)}) %collective-permute-start.1) | collective-permute-done | bytes 262176 | tf_op jit(solution)/shard_map/ppermute | solution.py:398
  38.1 3.1 %collective-permute-done.4.refs_2_ = bf16[64,1024]{1,0:T(8,128)(2,1)S(1)} collective-permute-done((bf16[64,1024]{1,0:T(8,128)(2,1)S(1)}, bf16[64,1024]{1,0:T(8,128)(2,1)S(1)}, u32[]{:S(2)}, u32[]{:S(2)}) %collective-permute-start.4) | collective-permute-done | bytes 131104 | tf_op jit(solution)/shard_map/ppermute | solution.py:404
  42.7 2.4 %collective-permute-start.9 = (bf16[64,1024]{1,0:T(8,128)(2,1)S(1)}, bf16[64,1024]{1,0:T(8,128)(2,1)S(1)}, u32[]{:S(2)}, u32[]{:S(2)}) collective-permute-start(bf16[64,1024]{1,0:T(8,128)(2,1)S(1)} %get-tuple-element.58), channel_id=1, source_target_pairs={{0,28},{4,24},{8,20},{12,16},{16,12},{20,8},{24,4},{28,0},{1,29},{... | collective-permute-start | bytes 393224 | tf_op jit(solution)/shard_map/ppermute | solution.py:404
  45.6 2.3 %collective-permute-done.8.refs_6_ = bf16[64,1024]{1,0:T(8,128)(2,1)S(1)} collective-permute-done((bf16[64,1024]{1,0:T(8,128)(2,1)S(1)}, bf16[64,1024]{1,0:T(8,128)(2,1)S(1)}, u32[]{:S(2)}, u32[]{:S(2)}) %collective-permute-start.8) | collective-permute-done | bytes 131104 | tf_op jit(solution)/shard_map/ppermute | solution.py:404
  47.8 3.4 %collective-permute-done.9.refs_7_ = bf16[64,1024]{1,0:T(8,128)(2,1)S(1)} collective-permute-done((bf16[64,1024]{1,0:T(8,128)(2,1)S(1)}, bf16[64,1024]{1,0:T(8,128)(2,1)S(1)}, u32[]{:S(2)}, u32[]{:S(2)}) %collective-permute-start.9) | collective-permute-done | bytes 131104 | tf_op jit(solution)/shard_map/ppermute | solution.py:404
  53.4 5.3 %shard_map.135 = (bf16[4,48,2304]{2,1,0:T(8,128)(2,1)S(1)}, bf16[4,48,2304]{2,1,0:T(8,128)(2,1)}) custom-call(bf16[8,48,1024]{2,1,0:T(8,128)(2,1)S(1)} %get-tuple-element.65.refs_0_.refs_1_, bf16[7168,1024]{1,0:T(8,128)(2,1)} %refs_1_.11, f32[8,128]{1,0:T(8,128)S(1)} %get-tuple-element.60.refs_2_.refs_0_.refs_5_), custom_call_target="tpu_custom_call" | custom-call | flops 1811939328 | bytes 6488064 | tf_op jit(solution)/shard_map/pallas_call | solution.py:40
  58.7 4.5 %shard_map.136 = (bf16[4,48,2304]{2,1,0:T(8,128)(2,1)S(1)}, bf16[4,48,2304]{2,1,0:T(8,128)(2,1)S(1)}) custom-call(bf16[8,48,1024]{2,1,0:T(8,128)(2,1)S(1)} %get-tuple-element.65.refs_0_.refs_1_, bf16[7168,1024]{1,0:T(8,128)(2,1)} %refs_1_.11, bf16[2,48,7168]{2,1,0:T(8,128)(2,1)S(1)} %collective-permute-done.13.refs_2_.refs_7_.refs_6_, ...), custom_call_target="tpu_custom_call" | custom-call | flops 1811939328 | bytes 6488064 | tf_op jit(solution)/shard_map/pallas_call | solution.py:40
  63.3 5.9 %shard_map.137 = (bf16[4,48,2560]{2,1,0:T(8,128)(2,1)S(1)}, bf16[4,48,2560]{2,1,0:T(8,128)(2,1)S(1)}) custom-call(bf16[8,48,1024]{2,1,0:T(8,128)(2,1)S(1)} %get-tuple-element.65.refs_0_.refs_1_, bf16[7168,1024]{1,0:T(8,128)(2,1)} %refs_1_.11, bf16[2,48,7168]{2,1,0:T(8,128)(2,1)S(1)} %collective-permute-done.14.refs_2_.refs_8_.refs_7_, ...), custom_call_target="tpu_custom_call" | custom-call | flops 2013265920 | bytes 7208960 | tf_op jit(solution)/shard_map/pallas_call | solution.py:40
  70.5 2.2 %shard_map.138 = (bf16[2,48,2304]{2,1,0:T(8,128)(2,1)S(1)}, bf16[2,48,2304]{2,1,0:T(8,128)(2,1)S(1)}) custom-call(bf16[4,48,2304]{2,1,0:T(8,128)(2,1)S(1)} %get-tuple-element.71.refs_0_, bf16[4,48,2304]{2,1,0:T(8,128)(2,1)} %collective-permute-done.19.refs_1_, bf16[4,48,2560]{2,1,0:T(8,128)(2,1)S(1)} %get-tuple-element.69.refs_2_), custom_call_target="tpu_custom_call" | custom-call | flops 442368 | bytes 2654208 | tf_op jit(solution)/shard_map/pallas_call | solution.py:40
  77.8 3.3 %collective-permute-done.22.refs_1_ = bf16[2,48,2304]{2,1,0:T(8,128)(2,1)S(1)} collective-permute-done((bf16[2,48,2304]{2,1,0:T(8,128)(2,1)S(1)}, bf16[2,48,2304]{2,1,0:T(8,128)(2,1)S(1)}, u32[]{:S(2)}, u32[]{:S(2)}) %collective-permute-start.22) | collective-permute-done | bytes 442400 | tf_op jit(solution)/shard_map/ppermute | solution.py:395
  82.9 10.6 %collective-permute-done.21.refs_1_ = bf16[2,48,2304]{2,1,0:T(8,128)(2,1)S(1)} collective-permute-done((bf16[2,48,2304]{2,1,0:T(8,128)(2,1)S(1)}, bf16[2,48,2304]{2,1,0:T(8,128)(2,1)S(1)}, u32[]{:S(2)}, u32[]{:S(2)}) %collective-permute-start.21) | collective-permute-done | bytes 442400 | tf_op jit(solution)/shard_map/ppermute | solution.py:395
  97.5 7.5 %collective-permute-done.24.refs_1_ = bf16[1,48,2304]{2,1,0:T(8,128)(2,1)S(1)} collective-permute-done((bf16[1,48,2304]{2,1,0:T(8,128)(2,1)S(1)}, bf16[1,48,2304]{2,1,0:T(8,128)(2,1)S(1)}, u32[]{:S(2)}, u32[]{:S(2)}) %collective-permute-start.24) | collective-permute-done | bytes 221216 | tf_op jit(solution)/shard_map/ppermute | solution.py:395
  109.1 6.6 %collective-permute-done.27.refs_1_ = bf16[1,48,2304]{2,1,0:T(8,128)(2,1)S(1)} collective-permute-done((bf16[1,48,2304]{2,1,0:T(8,128)(2,1)S(1)}, bf16[1,48,2304]{2,1,0:T(8,128)(2,1)S(1)}, u32[]{:S(2)}, u32[]{:S(2)}) %collective-permute-start.27) | collective-permute-done | bytes 221216 | tf_op jit(solution)/shard_map/ppermute | solution.py:395
  119.4 7.1 %shard_map.151.refs_2_.refs_13_ = f32[384,1024]{1,0:T(8,128)S(1)} custom-call(f32[8,128]{1,0:T(8,128)S(1)} %get-tuple-element.60.refs_2_.refs_0_.refs_5_, bf16[1024,7168]{1,0:T(8,128)(2,1)} %refs_1_.14, bf16[1024,7168]{1,0:T(8,128)(2,1)} %refs_2_.5, bf16[2,48,7168]{2,1,0:T(8,128)(2,1)S(1)} %shard_map.132.refs_7_.refs_3_.refs_2_, ...), custom_call_target="tpu_custom_call" | custom-call | flops 3623878656 | bytes 14745600 | tf_op jit(solution)/shard_map/pallas_call | solution.py:40
  127.1 3.6 %collective-permute-done.29.refs_1_ = bf16[2,48,2560]{2,1,0:T(8,128)(2,1)S(1)} collective-permute-done((bf16[2,48,2560]{2,1,0:T(8,128)(2,1)S(1)}, bf16[2,48,2560]{2,1,0:T(8,128)(2,1)S(1)}, u32[]{:S(2)}, u32[]{:S(2)}) %collective-permute-start.29) | collective-permute-done | bytes 491552 | tf_op jit(solution)/shard_map/ppermute | solution.py:395
  131.1 7.3 %shard_map.154.refs_13_.refs_14_ = f32[384,1024]{1,0:T(8,128)S(1)} custom-call(f32[8,128]{1,0:T(8,128)S(1)} %get-tuple-element.60.refs_2_.refs_0_.refs_5_, bf16[1024,7168]{1,0:T(8,128)(2,1)} %refs_1_.14, bf16[1024,7168]{1,0:T(8,128)(2,1)} %refs_2_.5, bf16[2,48,7168]{2,1,0:T(8,128)(2,1)S(1)} %shard_map.132.refs_7_.refs_3_.refs_2_, ...), custom_call_target="tpu_custom_call" | custom-call | flops 3623878656 | bytes 14745600 | tf_op jit(solution)/shard_map/pallas_call | solution.py:40
  138.4 8.4 %shard_map.155 = (bf16[48,1024]{1,0:T(8,128)(2,1)S(1)}, bf16[48,1024]{1,0:T(8,128)(2,1)S(1)}, bf16[48,1024]{1,0:T(8,128)(2,1)S(1)}, bf16[48,1024]{1,0:T(8,128)(2...) custom-call(f32[8,128]{1,0:T(8,128)S(1)} %get-tuple-element.60.refs_, ...), custom_call_target="tpu_custom_call" | custom-call | flops 4026531840 | bytes 16384000 | tf_op jit(solution)/shard_map/pallas_call | solution.py:40
  154.5 3.9 %collective-permute-done.40.refs_7_ = bf16[48,1024]{1,0:T(8,128)(2,1)S(1)} collective-permute-done((bf16[48,1024]{1,0:T(8,128)(2,1)S(1)}, bf16[48,1024]{1,0:T(8,128)(2,1)S(1)}, u32[]{:S(2)}, u32[]{:S(2)}) %collective-permute-start.40) | collective-permute-done | bytes 98336 | tf_op jit(solution)/shard_map/ppermute | solution.py:404
  161.2 8.4 %shard_map.157 = (f32[7168,1024]{1,0:T(8,128)}, f32[8,128]{1,0:T(8,128)S(1)}) custom-call(f32[8,128]{1,0:T(8,128)S(1)} %get-tuple-element.60.refs_2_.refs_0_.refs_5_, bf16[8,48,1024]{2,1,0:T(8,128)(2,1)S(1)} %get-tuple-element.65.refs_0_.refs_1_, bf16[2,48,7168]{2,1,0:T(8,128)(2,1)S(1)} %shard_map.132.refs_7_.refs_3_.refs_2_, ...), custom_call_target="tpu_custom_call" | custom-call | flops 2818572288 | bytes 20185088 | tf_op jit(solution)/shard_map/pallas_call | solution.py:40
  171.5 2.5 %collective-permute-start.43 = (bf16[2,48,1024]{2,1,0:T(8,128)(2,1)S(1)}, bf16[2,48,1024]{2,1,0:T(8,128)(2,1)S(1)}, u32[]{:S(2)}, u32[]{:S(2)}) collective-permute-start(bf16[2,48,1024]{2,1,0:T(8,128)(2,1)S(1)} %get-tuple-element.96.refs_11_), channel_id=1, source_target_pairs={{0,2},{1,3},{2,0},{3,1},{4,6},{5,7},{6,4},{7,5},{8,10},{9,11},{10,... | collective-permute-start | bytes 589832 | tf_op jit(solution)/shard_map/ppermute | solution.py:398
  174.0 8.5 %shard_map.159 = (f32[7168,1024]{1,0:T(8,128)}, f32[8,128]{1,0:T(8,128)S(1)}) custom-call(f32[8,128]{1,0:T(8,128)S(1)} %get-tuple-element.60.refs_2_.refs_0_.refs_5_, bf16[8,48,1024]{2,1,0:T(8,128)(2,1)S(1)} %get-tuple-element.65.refs_0_.refs_1_, bf16[2,48,7168]{2,1,0:T(8,128)(2,1)S(1)} %shard_map.132.refs_7_.refs_3_.refs_2_, ...), custom_call_target="tpu_custom_call", output_to_operand_aliasing={{0}: (10, {})} | custom-call | flops 2818572288 | bytes 20185088 | tf_op jit(solution)/shard_map/pallas_call | solution.py:40
  183.5 2.5 %collective-permute-start.46 = (f32[48,128]{1,0:T(8,128)S(1)}, f32[48,128]{1,0:T(8,128)S(1)}, u32[]{:S(2)}, u32[]{:S(2)}) collective-permute-start(f32[48,128]{1,0:T(8,128)S(1)} %shard_map.161.refs_8_.refs_12_), channel_id=1, source_target_pairs={{0,3},{1,2},{2,1},{3,0},{4,7},{5,6},{6,5},{7,4},{8,11},{9,10},{10,... | collective-permute-start | bytes 73736 | tf_op jit(solution)/shard_map/ppermute | solution.py:398
  (123 shorter events, 56.8 us)
Async XLA Ops:
  4.9 46.3 %collective-permute-start.11 = (bf16[2,48,7168]{2,1,0:T(8,128)(2,1)S(1)}, bf16[2,48,7168]{2,1,0:T(8,128)(2,1)S(1)}, u32[]{:S(2)}, u32[]{:S(2)}) collective-permute-start(bf16[2,48,7168]{2,1,0:T(8,128)(2,1)S(1)} %shard_map.132.refs_7_.refs_3_.refs_2_), channel_id=1, source_target_pairs={{0,16},{4,12},{8,24},{12,4},{16,0},{20,28},{24,8},{28,20},{1,17},{... | collective-permute-start | bytes 4128776 | tf_op jit(solution)/shard_map/ppermute | solution.py:395
  5.0 46.2 %collective-permute-start.10 = (bf16[2,48,7168]{2,1,0:T(8,128)(2,1)S(1)}, bf16[2,48,7168]{2,1,0:T(8,128)(2,1)}, u32[]{:S(2)}, u32[]{:S(2)}) collective-permute-start(bf16[2,48,7168]{2,1,0:T(8,128)(2,1)S(1)} %shard_map.132.refs_7_.refs_3_.refs_2_), channel_id=1, source_target_pairs={{0,8},{4,20},{8,0},{12,28},{16,24},{20,4},{24,16},{28,12},{1,9},{5... | collective-permute-start | bytes 4128776 | tf_op jit(solution)/shard_map/ppermute | solution.py:395
  7.0 11.4 %collective-permute-start.2 = (bf16[64,2048]{1,0:T(8,128)(2,1)}, bf16[64,2048]{1,0:T(8,128)(2,1)S(1)}, u32[]{:S(2)}, u32[]{:S(2)}) collective-permute-start(bf16[64,2048]{1,0:T(8,128)(2,1)} %shard_map.131.refs_2_.refs_3_), channel_id=1, source_target_pairs={{0,3},{1,2},{2,1},{3,0},{4,7},{5,6},{6,5},{7,4},{8,11},{9,10},{10,... | collective-permute-start | bytes 786440 | tf_op jit(solution)/shard_map/ppermute | solution.py:398
  10.6 22.0 %collective-permute-start.1 = (bf16[64,2048]{1,0:T(8,128)(2,1)}, bf16[64,2048]{1,0:T(8,128)(2,1)S(1)}, u32[]{:S(2)}, u32[]{:S(2)}) collective-permute-start(bf16[64,2048]{1,0:T(8,128)(2,1)} %shard_map.131.refs_2_.refs_3_), channel_id=1, source_target_pairs={{0,2},{1,3},{2,0},{3,1},{4,6},{5,7},{6,4},{7,5},{8,10},{9,11},{10,... | collective-permute-start | bytes 786440 | tf_op jit(solution)/shard_map/ppermute | solution.py:398
  10.6 22.0 %collective-permute-start = (bf16[64,2048]{1,0:T(8,128)(2,1)}, bf16[64,2048]{1,0:T(8,128)(2,1)S(1)}, u32[]{:S(2)}, u32[]{:S(2)}) collective-permute-start(bf16[64,2048]{1,0:T(8,128)(2,1)} %shard_map.131.refs_2_.refs_3_), channel_id=1, source_target_pairs={{0,1},{1,0},{2,3},{3,2},{4,5},{5,4},{6,7},{7,6},{8,9},{9,8},{10,11... | collective-permute-start | bytes 786440 | tf_op jit(solution)/shard_map/ppermute | solution.py:398
  42.7 8.6 %collective-permute-start.9 = (bf16[64,1024]{1,0:T(8,128)(2,1)S(1)}, bf16[64,1024]{1,0:T(8,128)(2,1)S(1)}, u32[]{:S(2)}, u32[]{:S(2)}) collective-permute-start(bf16[64,1024]{1,0:T(8,128)(2,1)S(1)} %get-tuple-element.58), channel_id=1, source_target_pairs={{0,28},{4,24},{8,20},{12,16},{16,12},{20,8},{24,4},{28,0},{1,29},{... | collective-permute-start | bytes 393224 | tf_op jit(solution)/shard_map/ppermute | solution.py:404
  51.4 11.9 %collective-permute-start.15 = (bf16[2,48,7168]{2,1,0:T(8,128)(2,1)S(1)}, bf16[2,48,7168]{2,1,0:T(8,128)(2,1)S(1)}, u32[]{:S(2)}, u32[]{:S(2)}) collective-permute-start(bf16[2,48,7168]{2,1,0:T(8,128)(2,1)S(1)} %collective-permute-done.11.refs_9_.refs_5_.refs_4_), channel_id=1, source_target_pairs={{0,4},{4,0},{8,12},{12,8},{16,20},{20,16},{24,28},{28,24},{1,5},{5... | collective-permute-start | bytes 4128776 | tf_op jit(solution)/shard_map/ppermute | solution.py:391
  51.9 11.4 %collective-permute-start.14 = (bf16[2,48,7168]{2,1,0:T(8,128)(2,1)}, bf16[2,48,7168]{2,1,0:T(8,128)(2,1)S(1)}, u32[]{:S(2)}, u32[]{:S(2)}) collective-permute-start(bf16[2,48,7168]{2,1,0:T(8,128)(2,1)} %collective-permute-done.10.refs_8_.refs_4_.refs_3_), channel_id=1, source_target_pairs={{0,4},{4,0},{8,12},{12,8},{16,20},{20,16},{24,28},{28,24},{1,5},{5... | collective-permute-start | bytes 4128776 | tf_op jit(solution)/shard_map/ppermute | solution.py:391
  52.0 18.5 %collective-permute-start.12 = (bf16[2,48,7168]{2,1,0:T(8,128)(2,1)}, bf16[2,48,7168]{2,1,0:T(8,128)(2,1)S(1)}, u32[]{:S(2)}, u32[]{:S(2)}) collective-permute-start(bf16[2,48,7168]{2,1,0:T(8,128)(2,1)} %collective-permute-done.10.refs_8_.refs_4_.refs_3_), channel_id=1, source_target_pairs={{0,16},{4,12},{8,24},{12,4},{16,0},{20,28},{24,8},{28,20},{1,17},{... | collective-permute-start | bytes 4128776 | tf_op jit(solution)/shard_map/ppermute | solution.py:395
  58.7 11.8 %collective-permute-start.19 = (bf16[4,48,2304]{2,1,0:T(8,128)(2,1)}, bf16[4,48,2304]{2,1,0:T(8,128)(2,1)}, u32[]{:S(2)}, u32[]{:S(2)}) collective-permute-start(bf16[4,48,2304]{2,1,0:T(8,128)(2,1)} %get-tuple-element.66.refs_3_), channel_id=1, source_target_pairs={{0,4},{4,0},{8,12},{12,8},{16,20},{20,16},{24,28},{28,24},{1,5},{5... | collective-permute-start | bytes 2654216 | tf_op jit(solution)/shard_map/ppermute | solution.py:391
  70.5 25.6 %collective-permute-start.16 = (bf16[2,48,7168]{2,1,0:T(8,128)(2,1)S(1)}, bf16[2,48,7168]{2,1,0:T(8,128)(2,1)S(1)}, u32[]{:S(2)}, u32[]{:S(2)}) collective-permute-start(bf16[2,48,7168]{2,1,0:T(8,128)(2,1)S(1)} %collective-permute-done.12.refs_2_.refs_6_.refs_5_), channel_id=1, source_target_pairs={{0,4},{4,0},{8,12},{12,8},{16,20},{20,16},{24,28},{28,24},{1,5},{5... | collective-permute-start | bytes 4128776 | tf_op jit(solution)/shard_map/ppermute | solution.py:391
  75.7 18.0 %collective-permute-start.20 = (bf16[2,48,2560]{2,1,0:T(8,128)(2,1)S(1)}, bf16[2,48,2560]{2,1,0:T(8,128)(2,1)S(1)}, u32[]{:S(2)}, u32[]{:S(2)}) collective-permute-start(bf16[2,48,2560]{2,1,0:T(8,128)(2,1)S(1)} %get-tuple-element.75.refs_3_), channel_id=1, source_target_pairs={{0,8},{4,20},{8,0},{12,28},{16,24},{20,4},{24,16},{28,12},{1,9},{5... | collective-permute-start | bytes 1474568 | tf_op jit(solution)/shard_map/ppermute | solution.py:395
  75.9 17.5 %collective-permute-start.21 = (bf16[2,48,2304]{2,1,0:T(8,128)(2,1)S(1)}, bf16[2,48,2304]{2,1,0:T(8,128)(2,1)S(1)}, u32[]{:S(2)}, u32[]{:S(2)}) collective-permute-start(bf16[2,48,2304]{2,1,0:T(8,128)(2,1)S(1)} %get-tuple-element.73.refs_2_), channel_id=1, source_target_pairs={{0,8},{4,20},{8,0},{12,28},{16,24},{20,4},{24,16},{28,12},{1,9},{5... | collective-permute-start | bytes 1327112 | tf_op jit(solution)/shard_map/ppermute | solution.py:395
  81.3 14.8 %collective-permute-start.25 = (bf16[1,48,2304]{2,1,0:T(8,128)(2,1)S(1)}, bf16[1,48,2304]{2,1,0:T(8,128)(2,1)S(1)}, u32[]{:S(2)}, u32[]{:S(2)}) collective-permute-start(bf16[1,48,2304]{2,1,0:T(8,128)(2,1)S(1)} %get-tuple-element.78.refs_2_), channel_id=1, source_target_pairs={{0,16},{4,12},{8,24},{12,4},{16,0},{20,28},{24,8},{28,20},{1,17},{... | collective-permute-start | bytes 663560 | tf_op jit(solution)/shard_map/ppermute | solution.py:395
  94.0 11.2 %collective-permute-start.23 = (bf16[1,48,2560]{2,1,0:T(8,128)(2,1)S(1)}, bf16[1,48,2560]{2,1,0:T(8,128)(2,1)S(1)}, u32[]{:S(2)}, u32[]{:S(2)}) collective-permute-start(bf16[1,48,2560]{2,1,0:T(8,128)(2,1)S(1)} %get-tuple-element.81.refs_3_), channel_id=1, source_target_pairs={{0,16},{4,12},{8,24},{12,4},{16,0},{20,28},{24,8},{28,20},{1,17},{... | collective-permute-start | bytes 737288 | tf_op jit(solution)/shard_map/ppermute | solution.py:395
  95.5 9.5 %collective-permute-start.24 = (bf16[1,48,2304]{2,1,0:T(8,128)(2,1)S(1)}, bf16[1,48,2304]{2,1,0:T(8,128)(2,1)S(1)}, u32[]{:S(2)}, u32[]{:S(2)}) collective-permute-start(bf16[1,48,2304]{2,1,0:T(8,128)(2,1)S(1)} %get-tuple-element.79.refs_2_), channel_id=1, source_target_pairs={{0,16},{4,12},{8,24},{12,4},{16,0},{20,28},{24,8},{28,20},{1,17},{... | collective-permute-start | bytes 663560 | tf_op jit(solution)/shard_map/ppermute | solution.py:395
  96.3 9.1 %collective-permute-start.28 = (bf16[1,48,2304]{2,1,0:T(8,128)(2,1)S(1)}, bf16[1,48,2304]{2,1,0:T(8,128)(2,1)S(1)}, u32[]{:S(2)}, u32[]{:S(2)}) collective-permute-start(bf16[1,48,2304]{2,1,0:T(8,128)(2,1)S(1)} %shard_map.144.refs_2_.refs_0_), channel_id=1, source_target_pairs={{0,8},{4,20},{8,0},{12,28},{16,24},{20,4},{24,16},{28,12},{1,9},{5... | collective-permute-start | bytes 663560 | tf_op jit(solution)/shard_map/ppermute | solution.py:395
  105.6 11.1 %collective-permute-start.31 = (bf16[2,48,2304]{2,1,0:T(8,128)(2,1)S(1)}, bf16[2,48,2304]{2,1,0:T(8,128)(2,1)S(1)}, u32[]{:S(2)}, u32[]{:S(2)}) collective-permute-start(bf16[2,48,2304]{2,1,0:T(8,128)(2,1)S(1)} %shard_map.147.refs_2_.refs_0_), channel_id=1, source_target_pairs={{0,16},{4,12},{8,24},{12,4},{16,0},{20,28},{24,8},{28,20},{1,17},{... | collective-permute-start | bytes 1327112 | tf_op jit(solution)/shard_map/ppermute | solution.py:395
  107.1 8.8 %collective-permute-start.26 = (bf16[1,48,2560]{2,1,0:T(8,128)(2,1)S(1)}, bf16[1,48,2560]{2,1,0:T(8,128)(2,1)S(1)}, u32[]{:S(2)}, u32[]{:S(2)}) collective-permute-start(bf16[1,48,2560]{2,1,0:T(8,128)(2,1)S(1)} %shard_map.146.refs_2_.refs_0_), channel_id=1, source_target_pairs={{0,8},{4,20},{8,0},{12,28},{16,24},{20,4},{24,16},{28,12},{1,9},{5... | collective-permute-start | bytes 737288 | tf_op jit(solution)/shard_map/ppermute | solution.py:395
  107.4 8.4 %collective-permute-start.27 = (bf16[1,48,2304]{2,1,0:T(8,128)(2,1)S(1)}, bf16[1,48,2304]{2,1,0:T(8,128)(2,1)S(1)}, u32[]{:S(2)}, u32[]{:S(2)}) collective-permute-start(bf16[1,48,2304]{2,1,0:T(8,128)(2,1)S(1)} %shard_map.145.refs_2_.refs_0_), channel_id=1, source_target_pairs={{0,8},{4,20},{8,0},{12,28},{16,24},{20,4},{24,16},{28,12},{1,9},{5... | collective-permute-start | bytes 663560 | tf_op jit(solution)/shard_map/ppermute | solution.py:395
  117.0 9.6 %collective-permute-start.30 = (bf16[2,48,2304]{2,1,0:T(8,128)(2,1)S(1)}, bf16[2,48,2304]{2,1,0:T(8,128)(2,1)S(1)}, u32[]{:S(2)}, u32[]{:S(2)}) collective-permute-start(bf16[2,48,2304]{2,1,0:T(8,128)(2,1)S(1)} %shard_map.148.refs_2_.refs_0_), channel_id=1, source_target_pairs={{0,16},{4,12},{8,24},{12,4},{16,0},{20,28},{24,8},{28,20},{1,17},{... | collective-permute-start | bytes 1327112 | tf_op jit(solution)/shard_map/ppermute | solution.py:395
  118.1 12.6 %collective-permute-start.29 = (bf16[2,48,2560]{2,1,0:T(8,128)(2,1)S(1)}, bf16[2,48,2560]{2,1,0:T(8,128)(2,1)S(1)}, u32[]{:S(2)}, u32[]{:S(2)}) collective-permute-start(bf16[2,48,2560]{2,1,0:T(8,128)(2,1)S(1)} %shard_map.149.refs_2_.refs_0_), channel_id=1, source_target_pairs={{0,16},{4,12},{8,24},{12,4},{16,0},{20,28},{24,8},{28,20},{1,17},{... | collective-permute-start | bytes 1474568 | tf_op jit(solution)/shard_map/ppermute | solution.py:395
  159.8 11.6 %collective-permute-start.42 = (bf16[4,48,1024]{2,1,0:T(8,128)(2,1)S(1)}, bf16[4,48,1024]{2,1,0:T(8,128)(2,1)S(1)}, u32[]{:S(2)}, u32[]{:S(2)}) collective-permute-start(bf16[4,48,1024]{2,1,0:T(8,128)(2,1)S(1)} %get-tuple-element.93.refs_10_), channel_id=1, source_target_pairs={{0,1},{1,0},{2,3},{3,2},{4,5},{5,4},{6,7},{7,6},{8,9},{9,8},{10,11... | collective-permute-start | bytes 1179656 | tf_op jit(solution)/shard_map/ppermute | solution.py:398
  171.5 11.7 %collective-permute-start.43 = (bf16[2,48,1024]{2,1,0:T(8,128)(2,1)S(1)}, bf16[2,48,1024]{2,1,0:T(8,128)(2,1)S(1)}, u32[]{:S(2)}, u32[]{:S(2)}) collective-permute-start(bf16[2,48,1024]{2,1,0:T(8,128)(2,1)S(1)} %get-tuple-element.96.refs_11_), channel_id=1, source_target_pairs={{0,2},{1,3},{2,0},{3,1},{4,6},{5,7},{6,4},{7,5},{8,10},{9,11},{10,... | collective-permute-start | bytes 589832 | tf_op jit(solution)/shard_map/ppermute | solution.py:398
  (33 other events, 258.3 us)

commit v3 on v2

--- a/solution.py
+++ b/solution.py
@@ -138,7 +138,6 @@
     rows = [jnp.concatenate([row, pad], axis=1) for row in rows] + [jnp.zeros((6, LANES), F32)]
     rows = turn(jnp.concatenate(rows, axis=0))[0:own]
     factor = tokens * math.sqrt(width)
-    count = jnp.sum(column(rows, 1), axis=0, keepdims=True)
     root = lax.rsqrt(squares / width + epsilon)
     value = root * products
     dvalue = column(rows, 1) * (value - column(rows, 0)) * factor
@@ -151,18 +150,23 @@
                 pieces[d][0:own, part].astype(F32), token, heads[d][:, part]
             )
     for q, out in enumerate(outs):
-        out[0:own, :] = held_ref[q]
-        out[own:, :] = jnp.broadcast_to(count, (out.shape[0] - own, tile)).astype(BF16)
-
-
-def gather_kernel(*refs):
-    tiles, (out_ref, inverse_ref) = refs[:-2], refs[-2:]
-    own = out_ref.shape[1]
-    count = 0.0
-    for q, ref in enumerate(tiles):
-        out_ref[q] = ref[0:own, :]
-        count = count + ref[own : own + 16, 0:LANES].astype(F32)
-    inverse_ref[...] = 1.0 / count[0:8]
+        out[...] = held_ref[q]
+
+
+def pair_kernel(gate_ref, up_ref, live_ref, out_ref):
+    own, units = gate_ref.shape
+    out_ref[0, :, 0:units] = gate_ref[...]
+    out_ref[1, :, 0:units] = up_ref[...]
+    live = jnp.concatenate([live_ref[...].astype(F32), jnp.zeros((1, LANES - own), F32)], axis=1)
+    live = turn(jnp.concatenate([live, jnp.zeros((7, LANES), F32)], axis=0))[0:own].astype(BF16)
+    out_ref[0, :, units:] = live
+    out_ref[1, :, units:] = live
+
+
+def inverse_kernel(*refs):
+    total = functools.reduce(lambda a, b: a + b, [ref[0].astype(F32) for ref in refs[:-1]])
+    count = jnp.sum(column(total, 0), axis=0, keepdims=True)
+    refs[-1][...] = jnp.broadcast_to(1.0 / count, refs[-1].shape)
 
 
 def arrange_kernel(k, links, place_ref, *refs):
@@ -404,7 +408,6 @@
             came[reverse_links(q, links) if q % 2 else q] = lax.ppermute(tiles[q], "row", pairs)
         return [came[q] for q in range(rows)]
 
-    line = jax.ShapeDtypeStruct((8, LANES), F32)
     packed = call(
         pack_kernel,
         (1,),
@@ -417,7 +420,15 @@
     )
     pieces = [packed] + [along(packed, d) for d in range(1, cols)]
 
-    (paired,) = stack([gate_pre, up_pre], own, [2])
+    paired = call(
+        pair_kernel,
+        (1,),
+        [whole((own, units)), whole((own, units)), whole((1, own))],
+        whole((2, own, units + LANES)),
+        jax.ShapeDtypeStruct((2, own, units + LANES), BF16),
+        [gate_pre, up_pre, response_mask[None, :]],
+        cost=cost(0, own * units * 8),
+    )
     hop_a = linked(paired, 0)
     hop_b = linked(paired, 1)
 
@@ -426,22 +437,13 @@
         (1,),
         [smem, whole((1, own)), whole((1, own))]
         + [whole((own + 16, block))] * cols,
-        [whole((own + 16, tile))] * rows + [whole((own, LANES))],
-        [jax.ShapeDtypeStruct((own + 16, tile), BF16)] * rows + [jax.ShapeDtypeStruct((own, LANES), F32)],
+        [whole((own, tile))] * rows + [whole((own, LANES))],
+        [jax.ShapeDtypeStruct((own, tile), BF16)] * rows + [jax.ShapeDtypeStruct((own, LANES), F32)],
         [where, returns[None, :], response_mask[None, :], *pieces],
         scratch=[pltpu.VMEM((rows, own, tile), BF16)],
         cost=cost(own * width * 10, own * width * 4),
     )
-    d_out, inverse = call(
-        gather_kernel,
-        (1,),
-        [whole((own + 16, tile))] * rows,
-        [whole((rows, own, tile)), whole((8, LANES))],
-        [jax.ShapeDtypeStruct((rows, own, tile), BF16), line],
-        exchanged(tiles),
-        cost=cost(0, rows * own * tile * 4),
-        after=[hop_a, hop_b],
-    )
+    (d_out,) = stack(exchanged(tiles), own, [rows], after=[hop_a, hop_b])
 
     paired, hop_a, hop_b, d_out = lax.optimization_barrier((paired, hop_a, hop_b, d_out))
     held = [paired, hop_a, hop_b, linked(hop_a, 1)]
@@ -449,10 +451,10 @@
     for i in range(2, links):
         picks = picks + [tuple((at + len(held), j) for at, j in pair) for pair in picks]
         held = held + [linked(values, i) for values in held]
-    others = [across(values, 1) for values in held]
+    others = [across(values, 1) for values in held[:3]]
 
     lines = units // (2 * LANES)
-    sizes = [lines // 3, lines // 3]
+    sizes = [lines * 3 // 7, lines * 2 // 7]
     sizes = [size * 2 * LANES for size in sizes + [lines - sum(sizes)]]
     chunks = [(sum(sizes[:i]), size) for i, size in enumerate(sizes)]
     count = rows // 2
@@ -470,7 +472,7 @@
             [pl.BlockSpec((count, own, fb), lambda i: (0, 0, i))] * 2,
             [jax.ShapeDtypeStruct((count, own, extent), BF16)] * 2,
             [d_out, w_down],
-            limit=47,
+            limit=44,
             cost=cost(2 * rows * own * tile * extent, 2 * extent * tile + 2 * rows * own * extent),
             after=waits.get((number, 0), ()),
         )
@@ -527,13 +529,26 @@
         (1, 0): others[:1],
         (2, 0): others[1:3],
         (0, links): held[3:4],
-        (0, links + 1): others[3:4],
     }
     grads, total = {}, None
     chains = [reduced(number) for number in range(len(chunks))]
-    for _ in range(2 * links + 1):
+    for step in range(2 * links + 1):
         for chain in chains:
             next(chain)
+        if step == 0:
+            late, _ = lax.optimization_barrier((held[3:], ordered[0]))
+            others = others + [across(values, 1) for values in late]
+            waits[0, links + 1] = others[3:4]
+        if step == links + 1:
+            inverse = call(
+                inverse_kernel,
+                (1,),
+                [pl.BlockSpec((2, own, LANES), lambda i: (0, 0, units // LANES))] * (2 * len(held)),
+                whole((8, LANES)),
+                jax.ShapeDtypeStruct((8, LANES), F32),
+                [*held, *others],
+                cost=cost(0, rows * own * LANES * 4),
+            )
     next(chains[0])
     total = normed(0, total)
     for chain in chains[1:]:

time: 194 us -> 192 us (0.990)
  Pallas kernels: 67.8 us -> 62.3 us
  waiting for transfers between devices: 75.4 us -> 80.6 us
  starting transfers between devices: 45.2 us -> 43.2 us
    pallas_call x32 -> x33, Pallas kernels: 67.8 us -> 62.3 us  [call(): pl.pallas_call(body, grid=grid, in_specs=list(ins) + [pl.BlockSpec(memory...]
    ppermute x15, waiting for transfers between devices: 32.6 us -> 36.8 us  [linked(): return lax.ppermute(values, 'row', pairs)]
    ppermute x10, waiting for transfers between devices: 1.02 us -> 4.51 us  [across(): return lax.ppermute(values, 'row', [(r, r ^ bit) for r in range(rows)])]
    ppermute x15, starting transfers between devices: 17.4 us -> 15.1 us  [linked(): return lax.ppermute(values, 'row', pairs)]
  transfers between devices with their start and end apart: 47 -> 47, of which waited for: 24 -> 27; matrix products, arithmetic and copies ran while one was open for 0% -> 0% of each run, Pallas kernels for 29% -> 27%
where the time goes in v3:
time: 192 us; the launch traced here: 190 us
  waiting for transfers between devices  80.6 us (42%)
  Pallas kernels  62.3 us (32%)
  starting transfers between devices  43.2 us (22%)
  local copies, waits for them, and re-layouts  2.88 us (2%)
    pallas_call x33, Pallas kernels, call(): pl.pallas_call(body, grid=grid, in_specs=list(ins) + [pl.BlockSpec(memory...  62.3 us
    ppermute x15, waiting for transfers between devices, linked(): return lax.ppermute(values, 'row', pairs)  36.8 us
    ppermute x8, waiting for transfers between devices, along(): return lax.ppermute(values, 'col', [(c, c ^ bit) for c in range(cols)])  25.1 us
    ppermute x15, starting transfers between devices, linked(): return lax.ppermute(values, 'row', pairs)  15.1 us
    ppermute x14, waiting for transfers between devices, exchanged(): lax.ppermute(tiles[q], 'row', pairs)  14.2 us
    ppermute x8, starting transfers between devices, along(): return lax.ppermute(values, 'col', [(c, c ^ bit) for c in range(cols)])  13.4 us
    ppermute x14, starting transfers between devices, exchanged(): lax.ppermute(tiles[q], 'row', pairs)  12.7 us
    ppermute x10, waiting for transfers between devices, across(): return lax.ppermute(values, 'row', [(r, r ^ bit) for r in range(rows)])  4.51 us
  transfers between devices with their start and end apart: 47, of which 27 were waited for; matrix products, arithmetic and copies ran while one was open for 0% of the time, Pallas kernels for 27%

profile of v3, /device:TPU:4, one launch (start us, length us, event | category | flops | bytes accessed | tf_op | source)
XLA Modules:
  0.0 190.1 jit_solution(7879378715190074126)
XLA Ops:
  7.4 3.6 %collective-permute-start.4 = (bf16[64,2048]{1,0:T(8,128)(2,1)}, bf16[64,2048]{1,0:T(8,128)(2,1)S(1)}, u32[]{:S(2)}, u32[]{:S(2)}) collective-permute-start(bf16[64,2048]{1,0:T(8,128)(2,1)} %shard_map.131.refs_3_), channel_id=1, source_target_pairs={{0,3},{1,2},{2,1},{3,0},{4,7},{5,6},{6,5},{7,4},{8,11},{9,10},{10,... | collective-permute-start | bytes 786440 | tf_op jit(solution)/shard_map/ppermute | solution.py:402
  11.8 6.9 %collective-permute-done.4.refs_6_ = bf16[64,2048]{1,0:T(8,128)(2,1)S(1)} collective-permute-done((bf16[64,2048]{1,0:T(8,128)(2,1)}, bf16[64,2048]{1,0:T(8,128)(2,1)S(1)}, u32[]{:S(2)}, u32[]{:S(2)}) %collective-permute-start.4) | collective-permute-done | bytes 262176 | tf_op jit(solution)/shard_map/ppermute | solution.py:402
  18.7 14.2 %collective-permute-done.3.refs_5_ = bf16[64,2048]{1,0:T(8,128)(2,1)S(1)} collective-permute-done((bf16[64,2048]{1,0:T(8,128)(2,1)}, bf16[64,2048]{1,0:T(8,128)(2,1)S(1)}, u32[]{:S(2)}, u32[]{:S(2)}) %collective-permute-start.3) | collective-permute-done | bytes 262176 | tf_op jit(solution)/shard_map/ppermute | solution.py:402
  38.5 2.4 %collective-permute-done.6.refs_2_ = bf16[48,1024]{1,0:T(8,128)(2,1)S(1)} collective-permute-done((bf16[48,1024]{1,0:T(8,128)(2,1)S(1)}, bf16[48,1024]{1,0:T(8,128)(2,1)S(1)}, u32[]{:S(2)}, u32[]{:S(2)}) %collective-permute-start.6) | collective-permute-done | bytes 98336 | tf_op jit(solution)/shard_map/ppermute | solution.py:408
  42.4 2.4 %collective-permute-start.11 = (bf16[48,1024]{1,0:T(8,128)(2,1)S(1)}, bf16[48,1024]{1,0:T(8,128)(2,1)S(1)}, u32[]{:S(2)}, u32[]{:S(2)}) collective-permute-start(bf16[48,1024]{1,0:T(8,128)(2,1)S(1)} %get-tuple-element.57), channel_id=1, source_target_pairs={{0,28},{4,24},{8,20},{12,16},{16,12},{20,8},{24,4},{28,0},{1,29},{... | collective-permute-start | bytes 294920 | tf_op jit(solution)/shard_map/ppermute | solution.py:408
  46.9 2.7 %collective-permute-done.11.refs_7_ = bf16[48,1024]{1,0:T(8,128)(2,1)S(1)} collective-permute-done((bf16[48,1024]{1,0:T(8,128)(2,1)S(1)}, bf16[48,1024]{1,0:T(8,128)(2,1)S(1)}, u32[]{:S(2)}, u32[]{:S(2)}) %collective-permute-start.11) | collective-permute-done | bytes 98336 | tf_op jit(solution)/shard_map/ppermute | solution.py:408
  51.2 5.3 %shard_map.135 = (bf16[4,48,3072]{2,1,0:T(8,128)(2,1)S(1)}, bf16[4,48,3072]{2,1,0:T(8,128)(2,1)S(1)}) custom-call(bf16[8,48,1024]{2,1,0:T(8,128)(2,1)S(1)} %shard_map.134.refs_0_.refs_2_.refs_1_, bf16[7168,1024]{1,0:T(8,128)(2,1)} %refs_1_.11, bf16[8,48,1024]{2,1,0:T(8,128)(2,1)S(1)} %shard_map.134.refs_0_.refs_2_.refs_1_), custom_call_target="tpu_custom_call" | custom-call | flops 2415919104 | bytes 8650752 | tf_op jit(solution)/shard_map/pallas_call | solution.py:40
  56.6 3.7 %shard_map.136 = (bf16[4,48,2048]{2,1,0:T(8,128)(2,1)S(1)}, bf16[4,48,2048]{2,1,0:T(8,128)(2,1)S(1)}) custom-call(bf16[8,48,1024]{2,1,0:T(8,128)(2,1)S(1)} %shard_map.134.refs_0_.refs_2_.refs_1_, bf16[7168,1024]{1,0:T(8,128)(2,1)} %refs_1_.11, bf16[2,48,7296]{2,1,0:T(8,128)(2,1)S(1)} %collective-permute-done.13.refs_2_.refs_4_.refs_7_.refs_6_, ...), custom_call_target="tpu_custom_call" | custom-call | flops 1610612736 | bytes 5767168 | tf_op jit(solution)/shard_map/pallas_call | solution.py:40
  60.4 3.7 %shard_map.137 = (bf16[4,48,2048]{2,1,0:T(8,128)(2,1)S(1)}, bf16[4,48,2048]{2,1,0:T(8,128)(2,1)S(1)}) custom-call(bf16[8,48,1024]{2,1,0:T(8,128)(2,1)S(1)} %shard_map.134.refs_0_.refs_2_.refs_1_, bf16[7168,1024]{1,0:T(8,128)(2,1)} %refs_1_.11, bf16[2,48,7296]{2,1,0:T(8,128)(2,1)S(1)} %collective-permute-done.14.refs_2_.refs_5_.refs_8_.refs_7_, ...), custom_call_target="tpu_custom_call" | custom-call | flops 1610612736 | bytes 5767168 | tf_op jit(solution)/shard_map/pallas_call | solution.py:40
  64.1 4.9 %collective-permute-done.12.refs_2_.refs_3_.refs_6_.refs_5_ = bf16[2,48,7296]{2,1,0:T(8,128)(2,1)S(1)} collective-permute-done((bf16[2,48,7296]{2,1,0:T(8,128)(2,1)}, bf16[2,48,7296]{2,1,0:T(8,128)(2,1)S(1)}, u32[]{:S(2)}, u32[]{:S(2)}) %collective-permute-start.12) | collective-permute-done | bytes 1400864 | tf_op jit(solution)/shard_map/ppermute | solution.py:399
  76.3 3.8 %collective-permute-done.22.refs_1_ = bf16[2,48,3072]{2,1,0:T(8,128)(2,1)S(1)} collective-permute-done((bf16[2,48,3072]{2,1,0:T(8,128)(2,1)S(1)}, bf16[2,48,3072]{2,1,0:T(8,128)(2,1)S(1)}, u32[]{:S(2)}, u32[]{:S(2)}) %collective-permute-start.22) | collective-permute-done | bytes 589856 | tf_op jit(solution)/shard_map/ppermute | solution.py:399
  81.5 4.4 %collective-permute-done.21.refs_1_ = bf16[2,48,2048]{2,1,0:T(8,128)(2,1)S(1)} collective-permute-done((bf16[2,48,2048]{2,1,0:T(8,128)(2,1)S(1)}, bf16[2,48,2048]{2,1,0:T(8,128)(2,1)S(1)}, u32[]{:S(2)}, u32[]{:S(2)}) %collective-permute-start.21) | collective-permute-done | bytes 393248 | tf_op jit(solution)/shard_map/ppermute | solution.py:399
  86.0 5.8 %collective-permute-done.20.refs_1_ = bf16[2,48,2048]{2,1,0:T(8,128)(2,1)S(1)} collective-permute-done((bf16[2,48,2048]{2,1,0:T(8,128)(2,1)S(1)}, bf16[2,48,2048]{2,1,0:T(8,128)(2,1)S(1)}, u32[]{:S(2)}, u32[]{:S(2)}) %collective-permute-start.20) | collective-permute-done | bytes 393248 | tf_op jit(solution)/shard_map/ppermute | solution.py:399
  95.0 4.6 %collective-permute-done.24.refs_1_ = bf16[1,48,2048]{2,1,0:T(8,128)(2,1)S(1)} collective-permute-done((bf16[1,48,2048]{2,1,0:T(8,128)(2,1)S(1)}, bf16[1,48,2048]{2,1,0:T(8,128)(2,1)S(1)}, u32[]{:S(2)}, u32[]{:S(2)}) %collective-permute-start.24) | collective-permute-done | bytes 196640 | tf_op jit(solution)/shard_map/ppermute | solution.py:399
  105.9 5.8 %collective-permute-done.27.refs_1_ = bf16[1,48,2048]{2,1,0:T(8,128)(2,1)S(1)} collective-permute-done((bf16[1,48,2048]{2,1,0:T(8,128)(2,1)S(1)}, bf16[1,48,2048]{2,1,0:T(8,128)(2,1)S(1)}, u32[]{:S(2)}, u32[]{:S(2)}) %collective-permute-start.27) | collective-permute-done | bytes 196640 | tf_op jit(solution)/shard_map/ppermute | solution.py:399
  111.8 4.1 %collective-permute-done.26.refs_1_ = bf16[1,48,2048]{2,1,0:T(8,128)(2,1)S(1)} collective-permute-done((bf16[1,48,2048]{2,1,0:T(8,128)(2,1)S(1)}, bf16[1,48,2048]{2,1,0:T(8,128)(2,1)S(1)}, u32[]{:S(2)}, u32[]{:S(2)}) %collective-permute-start.26) | collective-permute-done | bytes 196640 | tf_op jit(solution)/shard_map/ppermute | solution.py:399
  120.1 8.7 %shard_map.152.refs_2_.refs_13_ = f32[384,1024]{1,0:T(8,128)S(1)} custom-call(f32[8,128]{1,0:T(8,128)S(1)} %shard_map.147.refs_2_.refs_0_.refs_5_, bf16[1024,7168]{1,0:T(8,128)(2,1)} %refs_1_.14, bf16[1024,7168]{1,0:T(8,128)(2,1)} %refs_2_.5, bf16[2,48,7296]{2,1,0:T(8,128)(2,1)S(1)} %shard_map.132.refs_7_.refs_0_.refs_3_.refs_2_, ...), custom_call_target="tpu_custom_call" | custom-call | flops 4831838208 | bytes 19660800 | tf_op jit(solution)/shard_map/pallas_call | solution.py:40
  131.9 6.4 %shard_map.155.refs_13_.refs_14_ = f32[384,1024]{1,0:T(8,128)S(1)} custom-call(f32[8,128]{1,0:T(8,128)S(1)} %shard_map.147.refs_2_.refs_0_.refs_5_, bf16[1024,7168]{1,0:T(8,128)(2,1)} %refs_1_.14, bf16[1024,7168]{1,0:T(8,128)(2,1)} %refs_2_.5, bf16[2,48,7296]{2,1,0:T(8,128)(2,1)S(1)} %shard_map.132.refs_7_.refs_0_.refs_3_.refs_2_, ...), custom_call_target="tpu_custom_call" | custom-call | flops 3221225472 | bytes 13107200 | tf_op jit(solution)/shard_map/pallas_call | solution.py:40
  138.4 6.6 %shard_map.156 = (bf16[48,1024]{1,0:T(8,128)(2,1)S(1)}, bf16[48,1024]{1,0:T(8,128)(2,1)S(1)}, bf16[48,1024]{1,0:T(8,128)(2,1)S(1)}, bf16[48,1024]{1,0:T(8,128)(2...) custom-call(f32[8,128]{1,0:T(8,128)S(1)} %shard_map.147.refs_2_.refs, ...), custom_call_target="tpu_custom_call" | custom-call | flops 3221225472 | bytes 13107200 | tf_op jit(solution)/shard_map/pallas_call | solution.py:40
  152.7 2.9 %collective-permute-done.40.refs_7_ = bf16[48,1024]{1,0:T(8,128)(2,1)S(1)} collective-permute-done((bf16[48,1024]{1,0:T(8,128)(2,1)S(1)}, bf16[48,1024]{1,0:T(8,128)(2,1)S(1)}, u32[]{:S(2)}, u32[]{:S(2)}) %collective-permute-start.40) | collective-permute-done | bytes 98336 | tf_op jit(solution)/shard_map/ppermute | solution.py:408
  159.8 8.7 %shard_map.158 = (f32[7168,1024]{1,0:T(8,128)}, f32[8,128]{1,0:T(8,128)S(1)}) custom-call(f32[8,128]{1,0:T(8,128)S(1)} %shard_map.147.refs_2_.refs_0_.refs_5_, bf16[8,48,1024]{2,1,0:T(8,128)(2,1)S(1)} %shard_map.134.refs_0_.refs_2_.refs_1_, bf16[2,48,7296]{2,1,0:T(8,128)(2,1)S(1)} %shard_map.132.refs_7_.refs_0_.refs_3_.refs_2_, ...), custom_call_target="tpu_custom_call" | custom-call | flops 2818572288 | bytes 20185088 | tf_op jit(solution)/shard_map/pallas_call | solution.py:40
  169.5 2.8 %collective-permute-start.43 = (bf16[2,48,1024]{2,1,0:T(8,128)(2,1)S(1)}, bf16[2,48,1024]{2,1,0:T(8,128)(2,1)S(1)}, u32[]{:S(2)}, u32[]{:S(2)}) collective-permute-start(bf16[2,48,1024]{2,1,0:T(8,128)(2,1)S(1)} %get-tuple-element.94.refs_11_), channel_id=1, source_target_pairs={{0,2},{1,3},{2,0},{3,1},{4,6},{5,7},{6,4},{7,5},{8,10},{9,11},{10,... | collective-permute-start | bytes 589832 | tf_op jit(solution)/shard_map/ppermute | solution.py:402
  172.4 8.9 %shard_map.160 = (f32[7168,1024]{1,0:T(8,128)}, f32[8,128]{1,0:T(8,128)S(1)}) custom-call(f32[8,128]{1,0:T(8,128)S(1)} %shard_map.147.refs_2_.refs_0_.refs_5_, bf16[8,48,1024]{2,1,0:T(8,128)(2,1)S(1)} %shard_map.134.refs_0_.refs_2_.refs_1_, bf16[2,48,7296]{2,1,0:T(8,128)(2,1)S(1)} %shard_map.132.refs_7_.refs_0_.refs_3_.refs_2_, ...), custom_call_target="tpu_custom_call", output_to_operand_aliasing={{0}: (10, {})} | custom-call | flops 2818572288 | bytes 20185088 | tf_op jit(solution)/shard_map/pallas_call | solution.py:40
  181.5 2.8 %collective-permute-start.46 = (f32[48,128]{1,0:T(8,128)S(1)}, f32[48,128]{1,0:T(8,128)S(1)}, u32[]{:S(2)}, u32[]{:S(2)}) collective-permute-start(f32[48,128]{1,0:T(8,128)S(1)} %shard_map.162.refs_8_.refs_12_), channel_id=1, source_target_pairs={{0,3},{1,2},{2,1},{3,0},{4,7},{5,6},{6,5},{7,4},{8,11},{9,10},{10,... | collective-permute-start | bytes 73736 | tf_op jit(solution)/shard_map/ppermute | solution.py:402
  (124 shorter events, 62.9 us)
Async XLA Ops:
  5.3 44.3 %collective-permute-start.1 = (bf16[2,48,7296]{2,1,0:T(8,128)(2,1)S(1)}, bf16[2,48,7296]{2,1,0:T(8,128)(2,1)S(1)}, u32[]{:S(2)}, u32[]{:S(2)}) collective-permute-start(bf16[2,48,7296]{2,1,0:T(8,128)(2,1)S(1)} %shard_map.132.refs_7_.refs_0_.refs_3_.refs_2_), channel_id=1, source_target_pairs={{0,16},{4,12},{8,24},{12,4},{16,0},{20,28},{24,8},{28,20},{1,17},{... | collective-permute-start | bytes 4202504 | tf_op jit(solution)/shard_map/ppermute | solution.py:399
  5.4 44.2 %collective-permute-start = (bf16[2,48,7296]{2,1,0:T(8,128)(2,1)S(1)}, bf16[2,48,7296]{2,1,0:T(8,128)(2,1)}, u32[]{:S(2)}, u32[]{:S(2)}) collective-permute-start(bf16[2,48,7296]{2,1,0:T(8,128)(2,1)S(1)} %shard_map.132.refs_7_.refs_0_.refs_3_.refs_2_), channel_id=1, source_target_pairs={{0,8},{4,20},{8,0},{12,28},{16,24},{20,4},{24,16},{28,12},{1,9},{5... | collective-permute-start | bytes 4202504 | tf_op jit(solution)/shard_map/ppermute | solution.py:399
  7.4 11.4 %collective-permute-start.4 = (bf16[64,2048]{1,0:T(8,128)(2,1)}, bf16[64,2048]{1,0:T(8,128)(2,1)S(1)}, u32[]{:S(2)}, u32[]{:S(2)}) collective-permute-start(bf16[64,2048]{1,0:T(8,128)(2,1)} %shard_map.131.refs_3_), channel_id=1, source_target_pairs={{0,3},{1,2},{2,1},{3,0},{4,7},{5,6},{6,5},{7,4},{8,11},{9,10},{10,... | collective-permute-start | bytes 786440 | tf_op jit(solution)/shard_map/ppermute | solution.py:402
  11.0 22.0 %collective-permute-start.3 = (bf16[64,2048]{1,0:T(8,128)(2,1)}, bf16[64,2048]{1,0:T(8,128)(2,1)S(1)}, u32[]{:S(2)}, u32[]{:S(2)}) collective-permute-start(bf16[64,2048]{1,0:T(8,128)(2,1)} %shard_map.131.refs_3_), channel_id=1, source_target_pairs={{0,2},{1,3},{2,0},{3,1},{4,6},{5,7},{6,4},{7,5},{8,10},{9,11},{10,... | collective-permute-start | bytes 786440 | tf_op jit(solution)/shard_map/ppermute | solution.py:402
  11.0 22.0 %collective-permute-start.2 = (bf16[64,2048]{1,0:T(8,128)(2,1)}, bf16[64,2048]{1,0:T(8,128)(2,1)}, u32[]{:S(2)}, u32[]{:S(2)}) collective-permute-start(bf16[64,2048]{1,0:T(8,128)(2,1)} %shard_map.131.refs_3_), channel_id=1, source_target_pairs={{0,1},{1,0},{2,3},{3,2},{4,5},{5,4},{6,7},{7,6},{8,9},{9,8},{10,11... | collective-permute-start | bytes 786440 | tf_op jit(solution)/shard_map/ppermute | solution.py:402
  49.7 10.7 %collective-permute-start.15 = (bf16[2,48,7296]{2,1,0:T(8,128)(2,1)S(1)}, bf16[2,48,7296]{2,1,0:T(8,128)(2,1)S(1)}, u32[]{:S(2)}, u32[]{:S(2)}) collective-permute-start(bf16[2,48,7296]{2,1,0:T(8,128)(2,1)S(1)} %collective-permute-done.1.refs_9_.refs_2_.refs_5_.refs_4_), channel_id=1, source_target_pairs={{0,4},{4,0},{8,12},{12,8},{16,20},{20,16},{24,28},{28,24},{1,5},{5... | collective-permute-start | bytes 4202504 | tf_op jit(solution)/shard_map/ppermute | solution.py:395
  50.2 10.2 %collective-permute-start.14 = (bf16[2,48,7296]{2,1,0:T(8,128)(2,1)}, bf16[2,48,7296]{2,1,0:T(8,128)(2,1)S(1)}, u32[]{:S(2)}, u32[]{:S(2)}) collective-permute-start(bf16[2,48,7296]{2,1,0:T(8,128)(2,1)} %collective-permute-done.refs_8_.refs_1_.refs_4_.refs_3_), channel_id=1, source_target_pairs={{0,4},{4,0},{8,12},{12,8},{16,20},{20,16},{24,28},{28,24},{1,5},{5... | collective-permute-start | bytes 4202504 | tf_op jit(solution)/shard_map/ppermute | solution.py:395
  50.3 18.8 %collective-permute-start.12 = (bf16[2,48,7296]{2,1,0:T(8,128)(2,1)}, bf16[2,48,7296]{2,1,0:T(8,128)(2,1)S(1)}, u32[]{:S(2)}, u32[]{:S(2)}) collective-permute-start(bf16[2,48,7296]{2,1,0:T(8,128)(2,1)} %collective-permute-done.refs_8_.refs_1_.refs_4_.refs_3_), channel_id=1, source_target_pairs={{0,16},{4,12},{8,24},{12,4},{16,0},{20,28},{24,8},{28,20},{1,17},{... | collective-permute-start | bytes 4202504 | tf_op jit(solution)/shard_map/ppermute | solution.py:399
  56.6 13.1 %collective-permute-start.19 = (bf16[4,48,3072]{2,1,0:T(8,128)(2,1)S(1)}, bf16[4,48,3072]{2,1,0:T(8,128)(2,1)S(1)}, u32[]{:S(2)}, u32[]{:S(2)}) collective-permute-start(bf16[4,48,3072]{2,1,0:T(8,128)(2,1)S(1)} %get-tuple-element.63.refs_3_), channel_id=1, source_target_pairs={{0,4},{4,0},{8,12},{12,8},{16,20},{20,16},{24,28},{28,24},{1,5},{5... | collective-permute-start | bytes 3538952 | tf_op jit(solution)/shard_map/ppermute | solution.py:395
  69.1 22.7 %collective-permute-start.16 = (bf16[2,48,7296]{2,1,0:T(8,128)(2,1)S(1)}, bf16[2,48,7296]{2,1,0:T(8,128)(2,1)S(1)}, u32[]{:S(2)}, u32[]{:S(2)}) collective-permute-start(bf16[2,48,7296]{2,1,0:T(8,128)(2,1)S(1)} %collective-permute-done.12.refs_2_.refs_3_.refs_6_.refs_5_), channel_id=1, source_target_pairs={{0,4},{4,0},{8,12},{12,8},{16,20},{20,16},{24,28},{28,24},{1,5},{5... | collective-permute-start | bytes 4202504 | tf_op jit(solution)/shard_map/ppermute | solution.py:395
  70.2 9.9 %collective-permute-start.22 = (bf16[2,48,3072]{2,1,0:T(8,128)(2,1)S(1)}, bf16[2,48,3072]{2,1,0:T(8,128)(2,1)S(1)}, u32[]{:S(2)}, u32[]{:S(2)}) collective-permute-start(bf16[2,48,3072]{2,1,0:T(8,128)(2,1)S(1)} %get-tuple-element.70.refs_2_), channel_id=1, source_target_pairs={{0,8},{4,20},{8,0},{12,28},{16,24},{20,4},{24,16},{28,12},{1,9},{5... | collective-permute-start | bytes 1769480 | tf_op jit(solution)/shard_map/ppermute | solution.py:399
  73.8 12.1 %collective-permute-start.21 = (bf16[2,48,2048]{2,1,0:T(8,128)(2,1)S(1)}, bf16[2,48,2048]{2,1,0:T(8,128)(2,1)S(1)}, u32[]{:S(2)}, u32[]{:S(2)}) collective-permute-start(bf16[2,48,2048]{2,1,0:T(8,128)(2,1)S(1)} %get-tuple-element.71.refs_2_), channel_id=1, source_target_pairs={{0,8},{4,20},{8,0},{12,28},{16,24},{20,4},{24,16},{28,12},{1,9},{5... | collective-permute-start | bytes 1179656 | tf_op jit(solution)/shard_map/ppermute | solution.py:399
  75.1 16.6 %collective-permute-start.20 = (bf16[2,48,2048]{2,1,0:T(8,128)(2,1)S(1)}, bf16[2,48,2048]{2,1,0:T(8,128)(2,1)S(1)}, u32[]{:S(2)}, u32[]{:S(2)}) collective-permute-start(bf16[2,48,2048]{2,1,0:T(8,128)(2,1)S(1)} %get-tuple-element.73.refs_3_), channel_id=1, source_target_pairs={{0,8},{4,20},{8,0},{12,28},{16,24},{20,4},{24,16},{28,12},{1,9},{5... | collective-permute-start | bytes 1179656 | tf_op jit(solution)/shard_map/ppermute | solution.py:399
  80.5 11.4 %collective-permute-start.25 = (bf16[1,48,3072]{2,1,0:T(8,128)(2,1)S(1)}, bf16[1,48,3072]{2,1,0:T(8,128)(2,1)S(1)}, u32[]{:S(2)}, u32[]{:S(2)}) collective-permute-start(bf16[1,48,3072]{2,1,0:T(8,128)(2,1)S(1)} %get-tuple-element.76.refs_2_), channel_id=1, source_target_pairs={{0,16},{4,12},{8,24},{12,4},{16,0},{20,28},{24,8},{28,20},{1,17},{... | collective-permute-start | bytes 884744 | tf_op jit(solution)/shard_map/ppermute | solution.py:399
  92.0 10.6 %collective-permute-start.28 = (bf16[1,48,3072]{2,1,0:T(8,128)(2,1)S(1)}, bf16[1,48,3072]{2,1,0:T(8,128)(2,1)S(1)}, u32[]{:S(2)}, u32[]{:S(2)}) collective-permute-start(bf16[1,48,3072]{2,1,0:T(8,128)(2,1)S(1)} %shard_map.144.refs_2_.refs_0_), channel_id=1, source_target_pairs={{0,8},{4,20},{8,0},{12,28},{16,24},{20,4},{24,16},{28,12},{1,9},{5... | collective-permute-start | bytes 884744 | tf_op jit(solution)/shard_map/ppermute | solution.py:399
  93.5 8.3 %collective-permute-start.23 = (bf16[1,48,2048]{2,1,0:T(8,128)(2,1)S(1)}, bf16[1,48,2048]{2,1,0:T(8,128)(2,1)S(1)}, u32[]{:S(2)}, u32[]{:S(2)}) collective-permute-start(bf16[1,48,2048]{2,1,0:T(8,128)(2,1)S(1)} %get-tuple-element.79.refs_3_), channel_id=1, source_target_pairs={{0,16},{4,12},{8,24},{12,4},{16,0},{20,28},{24,8},{28,20},{1,17},{... | collective-permute-start | bytes 589832 | tf_op jit(solution)/shard_map/ppermute | solution.py:399
  102.8 14.1 %collective-permute-start.31 = (bf16[2,48,3072]{2,1,0:T(8,128)(2,1)S(1)}, bf16[2,48,3072]{2,1,0:T(8,128)(2,1)S(1)}, u32[]{:S(2)}, u32[]{:S(2)}) collective-permute-start(bf16[2,48,3072]{2,1,0:T(8,128)(2,1)S(1)} %shard_map.148.refs_2_.refs_0_), channel_id=1, source_target_pairs={{0,16},{4,12},{8,24},{12,4},{16,0},{20,28},{24,8},{28,20},{1,17},{... | collective-permute-start | bytes 1769480 | tf_op jit(solution)/shard_map/ppermute | solution.py:399
  103.8 7.8 %collective-permute-start.27 = (bf16[1,48,2048]{2,1,0:T(8,128)(2,1)S(1)}, bf16[1,48,2048]{2,1,0:T(8,128)(2,1)S(1)}, u32[]{:S(2)}, u32[]{:S(2)}) collective-permute-start(bf16[1,48,2048]{2,1,0:T(8,128)(2,1)S(1)} %shard_map.145.refs_2_.refs_0_), channel_id=1, source_target_pairs={{0,8},{4,20},{8,0},{12,28},{16,24},{20,4},{24,16},{28,12},{1,9},{5... | collective-permute-start | bytes 589832 | tf_op jit(solution)/shard_map/ppermute | solution.py:399
  104.3 11.6 %collective-permute-start.26 = (bf16[1,48,2048]{2,1,0:T(8,128)(2,1)S(1)}, bf16[1,48,2048]{2,1,0:T(8,128)(2,1)S(1)}, u32[]{:S(2)}, u32[]{:S(2)}) collective-permute-start(bf16[1,48,2048]{2,1,0:T(8,128)(2,1)S(1)} %shard_map.146.refs_8_.refs_0_), channel_id=1, source_target_pairs={{0,8},{4,20},{8,0},{12,28},{16,24},{20,4},{24,16},{28,12},{1,9},{5... | collective-permute-start | bytes 589832 | tf_op jit(solution)/shard_map/ppermute | solution.py:399
  117.3 12.4 %collective-permute-start.29 = (bf16[2,48,2048]{2,1,0:T(8,128)(2,1)S(1)}, bf16[2,48,2048]{2,1,0:T(8,128)(2,1)S(1)}, u32[]{:S(2)}, u32[]{:S(2)}) collective-permute-start(bf16[2,48,2048]{2,1,0:T(8,128)(2,1)S(1)} %shard_map.150.refs_2_.refs_0_), channel_id=1, source_target_pairs={{0,16},{4,12},{8,24},{12,4},{16,0},{20,28},{24,8},{28,20},{1,17},{... | collective-permute-start | bytes 1179656 | tf_op jit(solution)/shard_map/ppermute | solution.py:399
  118.4 10.9 %collective-permute-start.30 = (bf16[2,48,2048]{2,1,0:T(8,128)(2,1)S(1)}, bf16[2,48,2048]{2,1,0:T(8,128)(2,1)S(1)}, u32[]{:S(2)}, u32[]{:S(2)}) collective-permute-start(bf16[2,48,2048]{2,1,0:T(8,128)(2,1)S(1)} %shard_map.149.refs_2_.refs_0_), channel_id=1, source_target_pairs={{0,16},{4,12},{8,24},{12,4},{16,0},{20,28},{24,8},{28,20},{1,17},{... | collective-permute-start | bytes 1179656 | tf_op jit(solution)/shard_map/ppermute | solution.py:399
  129.9 8.4 %collective-permute-start.33 = (bf16[4,48,2048]{2,1,0:T(8,128)(2,1)S(1)}, bf16[4,48,2048]{2,1,0:T(8,128)(2,1)S(1)}, u32[]{:S(2)}, u32[]{:S(2)}) collective-permute-start(bf16[4,48,2048]{2,1,0:T(8,128)(2,1)S(1)} %shard_map.154.refs_14_.refs_11_), channel_id=1, source_target_pairs={{0,4},{4,0},{8,12},{12,8},{16,20},{20,16},{24,28},{28,24},{1,5},{5... | collective-permute-start | bytes 2359304 | tf_op jit(solution)/shard_map/ppermute | solution.py:395
  158.1 11.4 %collective-permute-start.42 = (bf16[4,48,1024]{2,1,0:T(8,128)(2,1)S(1)}, bf16[4,48,1024]{2,1,0:T(8,128)(2,1)S(1)}, u32[]{:S(2)}, u32[]{:S(2)}) collective-permute-start(bf16[4,48,1024]{2,1,0:T(8,128)(2,1)S(1)} %get-tuple-element.91.refs_10_), channel_id=1, source_target_pairs={{0,1},{1,0},{2,3},{3,2},{4,5},{5,4},{6,7},{7,6},{8,9},{9,8},{10,11... | collective-permute-start | bytes 1179656 | tf_op jit(solution)/shard_map/ppermute | solution.py:402
  169.5 11.7 %collective-permute-start.43 = (bf16[2,48,1024]{2,1,0:T(8,128)(2,1)S(1)}, bf16[2,48,1024]{2,1,0:T(8,128)(2,1)S(1)}, u32[]{:S(2)}, u32[]{:S(2)}) collective-permute-start(bf16[2,48,1024]{2,1,0:T(8,128)(2,1)S(1)} %get-tuple-element.94.refs_11_), channel_id=1, source_target_pairs={{0,2},{1,3},{2,0},{3,1},{4,6},{5,7},{6,4},{7,5},{8,10},{9,11},{10,... | collective-permute-start | bytes 589832 | tf_op jit(solution)/shard_map/ppermute | solution.py:402
  (33 other events, 243.0 us)
